TPU v7x, 128 devices: a whole 4x4x4 slice. The times are simulated.
128 devices in a mesh: gx: 16 (over y, x), gy: 8 (over z, core).
Axes of the slice: x: 4, y: 4, z: 4, core: 2. Of those that a mesh axis runs over, the one named last changes fastest.
Arguments:
- features: bfloat16 [128, 128, 2048], P('gx', 'gy'), may hold values from -6 to 6
- labels: int32 [128, 128, 32], P('gx', 'gy'), may hold values from 0 to 255
- lists: int32 [128, 256], P(('gx', 'gy')), may hold values from 0 to 8191, as said below
- home: int32 [8192], replicated, may hold values from 0 to 8191, as said below
- conv_first: bfloat16 [1728, 64], replicated, may hold values from -0.15625 to 0.15625
- conv_second: bfloat16 [1728, 64], replicated, may hold values from -0.15625 to 0.15625
- head_in: bfloat16 [64, 256], replicated, may hold values from -12 to 12
- head_out: bfloat16 [256, 128], replicated, may hold values from -0.375 to 0.375
Outputs:
- embeddings: bfloat16 [8192, 128], P(('gx', 'gy'))
Inputs may be any that keep to these rules, and one draw needn't show every extreme that they name: `lists`: entries of a row are distinct. Of one row's labels, at most 8 have segments whose home rows lie in one block of 64 rows, and that many is reached in every row. `home`: A permutation of the segments.
All inputs are finite; a program needn't handle non-finite values.
Results may differ from a plain program's by a relative error of at most 0.015.
Values may be sent and summed in bfloat16 or wider, within the bound.
No kernel may reach another device: no remote copies, remote signals or barrier semaphores. Data moves between devices by JAX's collectives and lax.ppermute only.
A program may use at most 128 MiB of HBM per device.

v0:
```python
import math

import jax
import jax.numpy as jnp
from jax import lax
from jax.sharding import PartitionSpec as P


def extended(block, sides, width):
    for axis, dim in sides:
        count = lax.axis_size(axis)
        forward = [(i, i + 1) for i in range(count - 1)]
        backward = [(target, source) for source, target in forward]
        low = lax.ppermute(
            lax.slice_in_dim(block, block.shape[dim] - width, None, axis=dim), axis, forward
        )
        high = lax.ppermute(lax.slice_in_dim(block, 0, width, axis=dim), axis, backward)
        block = jnp.concatenate([low, block, high], axis=dim)
    return block


def conv_padded(padded, weight, channels):
    rows_x = padded.shape[0] - 2
    rows_y = padded.shape[1] - 2
    depth = padded.shape[2] // channels
    deeper = jnp.pad(padded, ((0, 0), (0, 0), (channels, channels)))
    total = jnp.zeros((rows_x * rows_y * depth, channels), jnp.float32)
    for shift_x in range(3):
        for shift_y in range(3):
            slab = deeper[shift_x : shift_x + rows_x, shift_y : shift_y + rows_y].reshape(
                rows_x * rows_y, depth + 2, channels
            )
            stacked = jnp.concatenate(
                [slab[:, shift_z : shift_z + depth] for shift_z in range(3)], axis=2
            )
            stacked = stacked.reshape(rows_x * rows_y * depth, 3 * channels)
            start = (shift_x * 3 + shift_y) * 3 * channels
            total = total + jnp.dot(
                stacked, weight[start : start + 3 * channels], preferred_element_type=jnp.float32
            )
    return total.reshape(rows_x, rows_y, depth * channels)


def single_layer(volume, weight, channels):
    padded = extended(jnp.maximum(volume, 0), (("gx", 0), ("gy", 1)), 1)
    return (volume.astype(jnp.float32) + conv_padded(padded, weight, channels)).astype(jnp.bfloat16)


def local(features, labels, lists, home, conv_first, conv_second, head_in, head_out):
    size_x, size_y, merged = features.shape
    channels = conv_first.shape[1]
    depth = merged // channels
    first = single_layer(features, conv_first, channels)
    second = single_layer(first, conv_second, channels)
    voxels = size_x * size_y * depth
    block = math.gcd(voxels, 2048)
    blocks = voxels // block
    slots = lists.shape[1]
    flat = second.reshape(blocks, block, channels)
    flat_labels = labels.reshape(blocks, block)
    slot_ids = jnp.arange(slots, dtype=jnp.int32)

    def pool_step(carry, piece):
        sums, counts = carry
        feats, labs = piece
        member = labs[None, :] == slot_ids[:, None]
        sums = sums + jnp.dot(
            member.astype(jnp.bfloat16), feats, preferred_element_type=jnp.float32
        )
        counts = counts + jnp.sum(member.astype(jnp.float32), axis=1)
        return ((sums, counts), None)

    start_carry = (jnp.zeros((slots, channels), jnp.float32), jnp.zeros((slots,), jnp.float32))
    (slot_sums, slot_counts), unused = lax.scan(pool_step, start_carry, (flat, flat_labels))
    home_rows = home[lists[0]]
    segs = home.shape[0]
    table = jnp.zeros((segs, channels), jnp.float32).at[home_rows].add(slot_sums)
    table_counts = jnp.zeros((segs,), jnp.float32).at[home_rows].add(slot_counts)
    total, count = (
        lax.psum_scatter(table, ("gx", "gy"), scatter_dimension=0, tiled=True),
        lax.psum_scatter(table_counts, ("gx", "gy"), scatter_dimension=0, tiled=True),
    )
    means = total / jnp.maximum(count, 1.0)[:, None]
    hidden = jnp.maximum(
        jnp.dot(means.astype(jnp.bfloat16), head_in, preferred_element_type=jnp.float32), 0.0
    ).astype(jnp.bfloat16)
    return jnp.dot(hidden, head_out, preferred_element_type=jnp.float32).astype(jnp.bfloat16)


def solution(mesh):
    placed = (
        P("gx", "gy", None),
        P("gx", "gy", None),
        P(("gx", "gy"), None),
        P(),
        P(),
        P(),
        P(),
        P(),
    )
    return jax.shard_map(
        local, mesh=mesh, in_specs=placed, out_specs=P(("gx", "gy"), None), check_vma=False
    )
```

profile of v0, /device:TPU:1, one launch (start us, length us, event | category | flops | bytes accessed | tf_op | source)
XLA Modules:
  0.0 832.5 jit_solution(4159785197043309515)
XLA Ops:
  9.0 4.6 collective-permute-start
  15.0 3.9 collective-permute-start.3
  18.9 3.5 collective-permute-start.2
  25.0 2.0 fusion.66
  27.0 2.0 reshape.164
  29.0 2.3 fusion.64
  31.3 1.9 reshape.166
  33.2 2.3 fusion.63
  35.5 1.9 reshape.168
  37.5 2.3 fusion.62
  39.8 1.9 reshape.170
  41.7 2.3 fusion.61
  44.0 2.2 reshape.172
  46.2 2.3 fusion.60
  49.4 2.3 fusion.59
  52.6 2.3 fusion.58
  55.8 1.6 fusion.57
  57.4 2.4 reshape.180
  89.8 4.6 collective-permute-start.4
  94.4 1.7 gather_fusion
  96.3 1.9 collective-permute-start.7
  98.2 4.7 collective-permute-start.6
  105.5 2.0 fusion.65
  107.5 2.0 reshape.183
  109.5 2.3 fusion.55
  111.8 1.9 reshape.185
  113.7 2.3 fusion.54
  116.0 1.9 reshape.187
  118.0 2.3 fusion.53
  120.3 1.9 reshape.189
  122.2 2.3 fusion.52
  124.6 1.9 reshape.191
  126.5 2.3 fusion.51
  128.8 2.4 reshape.193
  131.1 2.3 fusion.50
  134.3 2.3 fusion.49
  137.5 2.0 fusion.48
  139.5 1.9 reshape.199
  166.7 1.8 convolution_add_fusion
  168.5 1.8 copy.16
  170.3 1.7 reshape.201
  172.0 1.6 add_convert_fusion
  174.6 1.8 while.13
  176.5 3.8 scatter_custom_fusion
  180.3 2.1 scatter_custom_fusion.1
  182.4 74.2 %all-reduce.2 = f32[8192]{0:T(1024)S(1)} all-reduce(f32[8192]{0:T(1024)S(1)} %scatter_custom_fusion.1), channel_id=3, replica_groups=mesh['gx'=16,'gy'=8] {'gx','gy'}, use_global_device_ids=true, to_apply=%region_6.7.clone | all-reduce | flops 8192 | bytes 65536
  256.7 567.0 %reduce-scatter.2.cloned.1.call-done = f32[64,64]{1,0:T(8,128)} async-done(((f32[8192,64]{1,0:T(8,128)}), f32[64,64]{1,0:T(8,128)}) %reduce-scatter.2.cloned.1.call-update) | async-done | bytes 16400 | tf_op jit(solution)/shard_map/reduce_scatter | solution.py:80
  823.8 1.7 fusion.15
  (189 shorter events, 71.1 us)
Async XLA Ops:
  6.5 817.2 %copy-start = (bf16[256,128]{1,0:T(8,128)(2,1)S(1)}, bf16[256,128]{1,0:T(8,128)(2,1)}, u32[]{:S(2)}) copy-start(bf16[256,128]{1,0:T(8,128)(2,1)} %param.17) | copy-start | bytes 196612
  6.5 15.9 %copy-start.52 = (s32[1,256]{1,0:T(1,128)S(1)}, s32[1,256]{1,0:T(1,128)}, u32[]{:S(2)}) copy-start(s32[1,256]{1,0:T(1,128)} %param.12) | copy-start | bytes 3076
  6.5 817.2 %reduce-scatter.2.cloned.1.call-start = ((), (), s32[]{:S(2)}) async-start(), calls=%async_computation.1 | async-start | bytes 4227072 | tf_op jit(solution)/shard_map/reduce_scatter | solution.py:80
  7.7 5.9 collective-permute-start.1
  9.0 5.9 collective-permute-start
  15.0 7.6 collective-permute-start.3
  18.9 5.0 collective-permute-start.2
  59.8 1.5 copy-start.36
  59.8 1.8 copy-start.37
  62.8 1.5 copy-start.39
  62.8 1.8 copy-start.40
  65.8 1.5 copy-start.30
  65.8 1.8 copy-start.31
  68.8 1.2 copy-start.23
  68.8 1.5 copy-start.24
  68.8 1.8 copy-start.25
  71.8 1.5 copy-start.18
  71.8 1.8 copy-start.19
  74.8 1.5 copy-start.12
  74.8 1.8 copy-start.13
  77.8 1.2 copy-start.5
  77.8 1.5 copy-start.6
  77.8 1.8 copy-start.7
  80.8 1.2 copy-start.2
  86.6 7.8 copy-start.1
  87.2 16.3 %copy-start.50 = (s32[8,16,32]{2,1,0:T(8,128)S(1)}, s32[8,16,32]{2,1,0:T(8,128)}, u32[]{:S(2)}) copy-start(s32[8,16,32]{2,1,0:T(8,128)} %param.11) | copy-start | bytes 49156
  88.5 7.7 collective-permute-start.5
  89.8 6.4 collective-permute-start.4
  96.3 7.3 collective-permute-start.7
  98.2 6.2 collective-permute-start.6
  141.5 1.5 copy-start.42
  141.5 1.8 copy-start.43
  144.5 1.5 copy-start.45
  144.5 1.8 copy-start.46
  147.4 1.5 copy-start.33
  147.4 1.8 copy-start.34
  150.3 1.5 copy-start.27
  150.3 1.8 copy-start.28
  153.3 1.5 copy-start.21
  153.3 1.8 copy-start.22
  156.2 1.5 copy-start.15
  156.2 1.8 copy-start.16
  159.1 1.5 copy-start.9
  159.1 1.8 copy-start.10
  162.0 1.5 copy-start.4
  172.0 2.6 copy-start.49
  172.0 2.7 copy-start.51
  180.3 643.5 %copy-start.53 = (bf16[64,256]{1,0:T(8,128)(2,1)S(1)}, bf16[64,256]{1,0:T(8,128)(2,1)}, u32[]{:S(2)}) copy-start(bf16[64,256]{1,0:T(8,128)(2,1)} %param.16) | copy-start | bytes 98308
  (15 other events, 18.3 us)
Sparse Core Ops, SparseCore 0:
  180.4 643.2 reduce-scatter.1
where the time goes:
time: 849 us; the launch traced here: 832 us
  waiting for transfers between devices  571 us (67%)
  local copies, waits for them, and re-layouts  96.2 us (11%)
  blocking collectives  74.2 us (9%)
  other arithmetic  33.6 us (4%)
  starting transfers between devices  25.8 us (3%)
  matrix products  17.4 us (2%)
  between operations  14.6 us (2%)
    reduce_scatter x1, waiting for transfers between devices, local(): lax.psum_scatter(table, ('gx', 'gy'), scatter_dimension=0, tiled=True)  567 us
    unnamed x1, blocking collectives  74.2 us
    slice x18, local copies, waits for them, and re-layouts, conv_padded(): slab[:, shift_z:shift_z + depth]  37 us
    reshape x18, local copies, waits for them, and re-layouts, conv_padded(): deeper[shift_x:shift_x + rows_x, shift_y:shift_y + rows_y]  30.9 us
    concatenate x18, other arithmetic, conv_padded(): jnp.concatenate([slab[:, shift_z:shift_z + depth] for shift_z in range(3)...  20.2 us
    ppermute x4, starting transfers between devices, extended(): lax.ppermute(lax.slice_in_dim(block, block.shape[dim] - width, None, axis...  17.4 us
  transfers between devices with their start and end apart: 9, of which 5 were waited for; matrix products, arithmetic and copies ran while one was open for 1% of the time, Pallas kernels for 0%

commit v1 on v0

v1 whole, which is shorter than its diff:
```python
import functools

import jax
import jax.numpy as jnp
from jax import lax
from jax.experimental import pallas as pl
from jax.experimental.pallas import tpu as pltpu
from jax.sharding import PartitionSpec as P

F32 = jnp.float32
BF16 = jnp.bfloat16
SX, SY, SZ, CH = 8, 16, 32, 64
LANES = SZ * CH
WIDE = LANES + 2 * CH
NB = 8
EX = SX + 4
FX = SX + 2
CAP = 8
VMEM = pl.BlockSpec(memory_space=pltpu.VMEM)
SMEM = pl.BlockSpec(memory_space=pltpu.SMEM)


def params(mb=40):
    return pltpu.CompilerParams(vmem_limit_bytes=mb * 2**20)


def iota(shape, dim):
    return lax.broadcasted_iota(jnp.int32, shape, dim)


def dot(a, b):
    return jnp.dot(a, b, preferred_element_type=F32)


def widen(rows):
    zero = jnp.zeros((rows.shape[0], CH), rows.dtype)
    return jnp.concatenate([zero, rows, zero], axis=1)


def relu(rows):
    return jnp.maximum(rows, jnp.zeros_like(rows))


def band(w_ref, out_ref):
    zero = jnp.zeros((CH, CH), BF16)
    quiet = jnp.zeros((128, 128), BF16)
    for kx in range(3):
        for ky in range(3):
            start = (kx * 3 + ky) * 3 * CH
            w = w_ref[start : start + 3 * CH, :]
            both = jnp.concatenate(
                [jnp.concatenate([w, zero], axis=0), jnp.concatenate([zero, w], axis=0)], axis=1
            )
            base = kx * 384
            out_ref[ky, base : base + 256, 0:128] = both
            out_ref[ky, base + 128 : base + 384, 128:256] = both
            out_ref[ky, base + 256 : base + 384, 0:128] = quiet
            out_ref[ky, base : base + 128, 128:256] = quiet


def prepare_kernel(labels, lists, home, w1, w2, wb1, wb2, member, place, meta):
    slots = lists.shape[1]
    devices = home.shape[0]
    band(w1, wb1)
    band(w2, wb2)
    lab = labels[...].reshape(SX * SY, SZ).T
    ids = iota((slots, SX * SY), 0)
    count = jnp.zeros((slots, SX * SY), F32)
    for z in range(SZ):
        hit = jnp.broadcast_to(lab[z : z + 1, :], (slots, SX * SY)) == ids
        hot = hit.astype(F32)
        count = count + hot
        j, b = z % 4, z // 4
        member[j * slots : (j + 1) * slots, b * 128 : (b + 1) * 128] = hot.astype(BF16)
    count = jnp.sum(count, axis=1, keepdims=True)
    li = lists[...]
    rows = home.shape[0]
    which = (iota((rows, slots), 0) == jnp.broadcast_to(li >> 7, (rows, slots))).astype(BF16)
    table = home[...]
    high = (table >> 6).astype(F32).T.astype(BF16)
    low = (table & 63).astype(F32).T.astype(BF16)
    lane = iota((128, slots), 0) == jnp.broadcast_to(li & 127, (128, slots))
    owner = jnp.sum(jnp.where(lane, dot(high, which), 0.0), axis=0, keepdims=True)
    row = jnp.sum(jnp.where(lane, dot(low, which), 0.0), axis=0, keepdims=True)
    across = jnp.broadcast_to(owner, (slots, slots))
    same = (across.T == across) & (iota((slots, slots), 0) < iota((slots, slots), 1))
    rank = jnp.sum(same.astype(F32), axis=0, keepdims=True)
    at = (owner * CAP + rank).astype(jnp.int32)
    total = place.shape[0]
    place[...] = (iota((total, slots), 0) == jnp.broadcast_to(at, (total, slots))).astype(F32).astype(BF16)
    key = jnp.broadcast_to(row + 1.0, (128, slots)).T
    count = jnp.broadcast_to(count, (slots, 128))
    big = jnp.floor(count * (1.0 / 64.0))
    lanes = iota((slots, 128), 1)
    info = jnp.where(lanes == 64, key, 0.0)
    info = jnp.where(lanes == 65, big, info)
    info = jnp.where(lanes == 66, count - 64.0 * big, info)
    meta[...] = info.astype(BF16)


def prepare(labels, lists, home, w1, w2, devices):
    slots = lists.shape[1]
    return pl.pallas_call(
        prepare_kernel,
        out_shape=(
            jax.ShapeDtypeStruct((3, 1152, 256), BF16),
            jax.ShapeDtypeStruct((3, 1152, 256), BF16),
            jax.ShapeDtypeStruct((4 * slots, NB * SX * SY), BF16),
            jax.ShapeDtypeStruct((devices * CAP, slots), BF16),
            jax.ShapeDtypeStruct((slots, 128), BF16),
        ),
        in_specs=[VMEM] * 5,
        out_specs=(VMEM,) * 5,
        compiler_params=params(),
        cost_estimate=pl.CostEstimate(flops=10**8, bytes_accessed=8 * 2**20, transcendentals=0),
        name="prepare",
    )(labels, lists, home, w1, w2)


def choose(flag, yes, no):
    return jnp.where(flag, yes.astype(F32), no.astype(F32)).astype(BF16)


def x_extended(even, v, xa, xb):
    a = xa[...]
    b = xb[...]
    low = choose(even, b, a)
    high = choose(even, a, b)
    return jnp.concatenate([low, v[...], high], axis=0)


def columns_kernel(where, v, xa, xb, near, far):
    x_even = where[0] % 2 == 0
    y_even = where[1] % 2 == 0
    block = x_extended(x_even, v, xa, xb).reshape(EX * SY, LANES)
    r = iota((64, EX * SY), 0)
    c = r // 16
    y = jnp.where(c < 2, c, c + 12)
    pick = ((r % 16) * 16 + y == iota((64, EX * SY), 1)).astype(F32).astype(BF16)
    cols = dot(pick, block).astype(BF16)

    @pl.when(y_even)
    def _():
        near[...] = cols[32:64]
        far[...] = cols[0:32]

    @pl.when(jnp.logical_not(y_even))
    def _():
        near[...] = cols[0:32]
        far[...] = cols[32:64]


def columns(where, v, xa, xb):
    shape = jax.ShapeDtypeStruct((32, LANES), BF16)
    return pl.pallas_call(
        columns_kernel,
        out_shape=(shape, shape),
        in_specs=[SMEM, VMEM, VMEM, VMEM],
        out_specs=(VMEM, VMEM),
        compiler_params=params(),
        name="columns",
    )(where, v, xa, xb)


def windows(wide_ref, rows_out, pitch):
    parts = []
    for b in range(NB):
        parts.append(
            jnp.concatenate(
                [
                    wide_ref[kx * pitch : kx * pitch + rows_out, 256 * b : 256 * b + 384]
                    for kx in range(3)
                ],
                axis=1,
            )
        )
    return jnp.concatenate(parts, axis=0)


def blocks(rows):
    return jnp.concatenate([rows[:, 256 * b : 256 * b + 256] for b in range(NB)], axis=0)


def unblocks(stack):
    n = stack.shape[0] // NB
    return jnp.concatenate([stack[n * b : n * b + n] for b in range(NB)], axis=1)


def fold_y(below, same, above):
    n = same.shape[0]
    y = iota((n, 256), 0) % SY
    down = jnp.where(y == 0, 0.0, pltpu.roll(below, 1, 0))
    up = jnp.where(y == SY - 1, 0.0, pltpu.roll(above, n - 1, 0))
    return same + down + up


def inner_kernel(where, v, xa, xb, wb, out, wide):
    x_even = where[0] % 2 == 0
    block = x_extended(x_even, v, xa, xb).reshape(EX * SY, LANES)
    wide[...] = widen(relu(block))
    left = windows(wide, FX * SY, SY)
    conv = fold_y(dot(left, wb[0]), dot(left, wb[1]), dot(left, wb[2]))
    out[...] = conv + blocks(block[SY : SY + FX * SY]).astype(F32)


def inner(where, v, xa, xb, wb):
    return pl.pallas_call(
        inner_kernel,
        out_shape=jax.ShapeDtypeStruct((NB * FX * SY, 256), F32),
        in_specs=[SMEM, VMEM, VMEM, VMEM, VMEM],
        out_specs=VMEM,
        scratch_shapes=[pltpu.VMEM((EX * SY, WIDE), BF16)],
        compiler_params=params(),
        cost_estimate=pl.CostEstimate(flops=4 * 10**9, bytes_accessed=2 * 2**20, transcendentals=0),
        name="inner",
    )(where, v, xa, xb, wb)


def rolled(cols, kx):
    return cols if kx == 0 else pltpu.roll(cols, cols.shape[0] - kx, 0)


def spread(edge, count):
    return jnp.concatenate(
        [
            jnp.broadcast_to(edge[16 * b + x : 16 * b + x + 1, :], (SY, 256))
            for b in range(NB)
            for x in range(count)
        ],
        axis=0,
    )


def outer_kernel(
    where, part, near, far, ya, yb, wb1, wb2, member, place, meta, out, cols1, wide2, cols2
):
    gx, gy = where[0], where[1]
    last_x, last_y = where[2] - 1, where[3] - 1
    y_even = gy % 2 == 0
    own_low = choose(y_even, far[...], near[...])[0:16]
    own_high = choose(y_even, near[...], far[...])[16:32]
    low = choose(y_even, yb[...], ya[...])
    high = choose(y_even, ya[...], yb[...])
    edge = jnp.concatenate(
        [low[0:16], own_high, low[16:32], high[0:16], high[16:32], own_low], axis=0
    ).astype(F32)
    active = relu(edge)
    for kx in range(3):
        cols1[kx] = widen(rolled(active, kx).astype(BF16))

    def left(first, count):
        parts = []
        for b in range(NB):
            parts.append(
                jnp.concatenate(
                    [
                        cols1[kx, 16 * first : 16 * (first + count), 256 * b : 256 * b + 384]
                        for kx in range(3)
                    ],
                    axis=1,
                )
            )
        return jnp.concatenate(parts, axis=0)

    z0 = dot(left(0, 3), wb1[0]).reshape(NB, 48, 256)
    z1 = dot(left(2, 2), wb1[1]).reshape(NB, 32, 256)
    z2 = dot(left(3, 3), wb1[2]).reshape(NB, 48, 256)
    residual = rolled(edge, 1)
    x = iota((NB * 16, 256), 0) % 16 - 1
    inside = (x >= jnp.where(gx == 0, 0, -1)) & (x <= jnp.where(gx == last_x, SX - 1, SX))
    low_first = (
        (z0[:, 0:16] + z1[:, 0:16] + z2[:, 32:48]).reshape(NB * 16, 256) + blocks(residual[32:48])
    )
    high_first = (
        (z0[:, 16:32] + z1[:, 16:32] + z2[:, 16:32]).reshape(NB * 16, 256) + blocks(residual[48:64])
    )
    low_first = jnp.where(inside & (gy > 0), low_first, 0.0)
    high_first = jnp.where(inside & (gy < last_y), high_first, 0.0)
    from_low = z0[:, 32:48].reshape(NB * 16, 256)
    from_high = z2[:, 0:16].reshape(NB * 16, 256)

    n = NB * FX * SY
    row = iota((n, 256), 0)
    y = row % SY
    x = (row // SY) % FX - 1
    first = part[...]
    first = first + jnp.where(y == 0, spread(from_low, FX), 0.0)
    first = first + jnp.where(y == SY - 1, spread(from_high, FX), 0.0)
    inside = (x >= jnp.where(gx == 0, 0, -1)) & (x <= jnp.where(gx == last_x, SX - 1, SX))
    first = jnp.where(inside, first, 0.0).astype(BF16)
    wide2[...] = widen(relu(unblocks(first)))
    sides = relu(
        jnp.concatenate([unblocks(low_first), unblocks(high_first)], axis=0).astype(BF16)
    ).astype(F32)
    for kx in range(3):
        cols2[kx] = widen(rolled(sides, kx).astype(BF16))
    w0, w1, w2 = wb2[0], wb2[1], wb2[2]

    def side(first):
        parts = []
        for b in range(NB):
            parts.append(
                jnp.concatenate(
                    [cols2[kx, first : first + 16, 256 * b : 256 * b + 384] for kx in range(3)],
                    axis=1,
                )
            )
        return jnp.concatenate(parts, axis=0)

    left2 = windows(wide2, SX * SY, SY)
    conv = fold_y(dot(left2, w0), dot(left2, w1), dot(left2, w2))
    y = iota((NB * SX * SY, 256), 0) % SY
    conv = conv + jnp.where(y == 0, spread(dot(side(0), w0), SX), 0.0)
    conv = conv + jnp.where(y == SY - 1, spread(dot(side(16), w2), SX), 0.0)
    own = jnp.concatenate(
        [first[FX * SY * b + SY : FX * SY * b + SY + SX * SY] for b in range(NB)], axis=0
    )
    second = (own.astype(F32) + conv).astype(BF16)
    slots = meta.shape[0]
    a = dot(member[0 : 2 * slots, :], second[:, 0:128])
    c = dot(member[2 * slots : 4 * slots, :], second[:, 128:256])
    a = a + c
    lanes = iota((slots, 128), 1)
    sums = a[0:slots] + pltpu.roll(a[slots : 2 * slots], 64, 1)
    rows = jnp.where(lanes < CH, sums, meta[...].astype(F32)).astype(BF16)
    out[...] = dot(place[...], rows).astype(BF16)


def outer(where, part, near, far, ya, yb, wb1, wb2, member, place, meta):
    return pl.pallas_call(
        outer_kernel,
        out_shape=jax.ShapeDtypeStruct((place.shape[0], 128), BF16),
        in_specs=[SMEM] + [VMEM] * 10,
        out_specs=VMEM,
        scratch_shapes=[
            pltpu.VMEM((3, 96, WIDE), BF16),
            pltpu.VMEM((FX * SY, WIDE), BF16),
            pltpu.VMEM((3, 32, WIDE), BF16),
        ],
        compiler_params=params(),
        name="outer",
    )(where, part, near, far, ya, yb, wb1, wb2, member, place, meta)


def head_kernel(got, w_in, w_out, out):
    rows = got[...]
    n = rows.shape[0]
    seg = out.shape[0]
    unit = (iota((8, 128), 1) == CH).astype(F32).astype(BF16)
    key = lax.dot_general(unit, rows, (((1,), (1,)), ((), ())), preferred_element_type=F32)
    key = jnp.broadcast_to(key[0:1], (seg, n))
    hit = (key == (iota((seg, n), 0) + 1).astype(F32)).astype(F32).astype(BF16)
    total = dot(hit, rows)
    lanes = iota((seg, 128), 1)
    digits = jnp.where(lanes == CH + 1, total * 64.0, jnp.where(lanes == CH + 2, total, 0.0))
    count = jnp.sum(digits, axis=1, keepdims=True)
    means = (total[:, 0:CH] / jnp.maximum(count, 1.0)).astype(BF16)
    hidden = jnp.maximum(dot(means, w_in[...]), 0.0).astype(BF16)
    out[...] = dot(hidden, w_out[...]).astype(BF16)


def head(got, w_in, w_out, seg):
    return pl.pallas_call(
        head_kernel,
        out_shape=jax.ShapeDtypeStruct((seg, w_out.shape[1]), BF16),
        in_specs=[VMEM] * 3,
        out_specs=VMEM,
        compiler_params=params(),
        name="head",
    )(got, w_in, w_out)


def pairs(count):
    inner_pairs = [(i, i ^ 1) for i in range(count)]
    outer_pairs = [(i, i + 1 if i % 2 else i - 1) for i in range(1, count - 1)]
    return inner_pairs, outer_pairs


def local(n_gx, n_gy, features, labels, lists, home, conv_first, conv_second, head_in, head_out):
    gx = lax.axis_index("gx")
    gy = lax.axis_index("gy")
    devices = n_gx * n_gy
    where = jnp.stack([gx, gy, jnp.int32(n_gx), jnp.int32(n_gy)]).astype(jnp.int32)
    even = gx % 2 == 0
    to_a = lax.dynamic_slice_in_dim(features, jnp.where(even, SX - 2, 0), 2, 0)
    to_b = lax.dynamic_slice_in_dim(features, jnp.where(even, 0, SX - 2), 2, 0)
    inner_x, outer_x = pairs(n_gx)
    inner_y, outer_y = pairs(n_gy)
    xa = lax.ppermute(to_a, "gx", inner_x)
    xb = lax.ppermute(to_b, "gx", outer_x)
    wb1, wb2, member, place, meta = prepare(
        labels, lists, home.reshape(-1, 128), conv_first, conv_second, devices
    )
    near, far = columns(where, features, xa, xb)
    ya = lax.ppermute(near, "gy", inner_y)
    yb = lax.ppermute(far, "gy", outer_y)
    part = inner(where, features, xa, xb, wb1)
    rows = outer(where, part, near, far, ya, yb, wb1, wb2, member, place, meta)
    rows = rows.reshape(devices, CAP, 128)
    got = lax.all_to_all(rows, ("gx", "gy"), 0, 0, tiled=True)
    return head(got.reshape(devices * CAP, 128), head_in, head_out, home.shape[0] // devices)


def solution(mesh):
    placed = (
        P("gx", "gy", None),
        P("gx", "gy", None),
        P(("gx", "gy"), None),
        P(),
        P(),
        P(),
        P(),
        P(),
    )
    return jax.shard_map(
        functools.partial(local, mesh.shape["gx"], mesh.shape["gy"]),
        mesh=mesh,
        in_specs=placed,
        out_specs=P(("gx", "gy"), None),
        check_vma=False,
    )
```

time: 849 us -> 48.7 us (0.06); the launches traced: 832 us -> 48.4 us
  waiting for transfers between devices: 571 us -> 0.01 us
  local copies, waits for them, and re-layouts: 96.2 us -> 3.49 us
  blocking collectives: 74.2 us -> 20.4 us
  other arithmetic: 33.6 us -> 0.08 us
  matrix products: 17.4 us -> 0 us
  starting transfers between devices: 25.8 us -> 10 us
  between operations: 14.6 us -> 0.14 us
  Pallas kernels: 0 us -> 14.3 us
    reduce_scatter x1 -> x0, waiting for transfers between devices: 567 us -> none  [local(): lax.psum_scatter(table, ('gx', 'gy'), scatter_dimension=0, tiled=True)]
    unnamed x1 -> x0, blocking collectives: 74.2 us -> none
    slice x22 -> x0, local copies, waits for them, and re-layouts: 41 us -> none  [the longest x18 37 us: conv_padded(): slab[:, shift_z:shift_z + depth]]
    reshape x22 -> x0, local copies, waits for them, and re-layouts: 34.3 us -> none  [the longest x18 30.9 us: conv_padded(): deeper[shift_x:shift_x + rows_x, shift_y:shift_y + rows_y]]
    concatenate x20 -> x0, other arithmetic: 22.4 us -> none  [the longest x18 20.2 us: conv_padded(): jnp.concatenate([slab[:, shift_z:shift_z + depth] for shift_z in range(3)...]
    all_to_all x0 -> x1, blocking collectives: none -> 20.4 us  [local(): got = lax.all_to_all(rows, ('gx', 'gy'), 0, 0, tiled=True)]
    dot_general x21 -> x0, matrix products: 17.4 us -> none  [the longest x18 14.7 us: conv_padded(): jnp.dot(stacked, weight[start:start + 3 * channels], preferred_element_ty...]
    ppermute x8 -> x4, starting transfers between devices: 25.8 us -> 10 us  [the longest x1 4.57 us: local(): xa = lax.ppermute(to_a, 'gx', inner_x)]
  transfers between devices with their start and end apart: 9 -> 4, of which waited for: 5 -> 0; matrix products, arithmetic and copies ran while one was open for 1% -> 5% of each run, Pallas kernels for 0% -> 10%
where the time goes in v1:
time: 48.7 us; the launch traced here: 48.4 us
  blocking collectives  20.4 us (42%)
  Pallas kernels  14.3 us (29%)
  starting transfers between devices  10 us (21%)
  local copies, waits for them, and re-layouts  3.49 us (7%)
    all_to_all x1, blocking collectives, local(): got = lax.all_to_all(rows, ('gx', 'gy'), 0, 0, tiled=True)  20.4 us
    pallas_call x1, Pallas kernels, outer(): pl.pallas_call(outer_kernel, out_shape=jax.ShapeDtypeStruct((place.shape[...  7.44 us
    ppermute x1, starting transfers between devices, local(): xa = lax.ppermute(to_a, 'gx', inner_x)  4.57 us
    ppermute x1, starting transfers between devices, local(): yb = lax.ppermute(far, 'gy', outer_y)  3.44 us
    pallas_call x1, Pallas kernels, inner(): pl.pallas_call(inner_kernel, out_shape=jax.ShapeDtypeStruct((NB * FX * SY...  3.35 us
    unnamed x14, local copies, waits for them, and re-layouts  2.44 us
    pallas_call x1, Pallas kernels, prepare(): pl.pallas_call(prepare_kernel, out_shape=(jax.ShapeDtypeStruct((3, 1152,...  1.47 us
    ppermute x1, starting transfers between devices, local(): ya = lax.ppermute(near, 'gy', inner_y)  1.32 us
  transfers between devices with their start and end apart: 4, of which 0 were waited for; matrix products, arithmetic and copies ran while one was open for 5% of the time, Pallas kernels for 10%

profile of v1, /device:TPU:1, one launch (start us, length us, event | category | flops | bytes accessed | tf_op | source)
XLA Modules:
  0.0 48.4 jit_solution(14775176169034391969)
XLA Ops:
  0.0 0.0 copy-start
  0.0 0.0 copy-start.3
  0.0 0.0 copy-start.5
  0.0 0.0 copy-start.1
  0.0 1.0 %constant_dynamic-slice_fusion = (bf16[2,16,2048]{2,1,0:T(8,128)(2,1)S(1)}, bf16[2,16,2048]{2,1,0:T(8,128)(2,1)S(1)}) fusion(bf16[8,16,2048]{2,1,0:T(8,128)(2,1)} %v.3, s32[]{:T(128)S(6)} %select_n.18, s32[]{:T(128)S(6)} %select_n.17), kind=kLoop, calls=%fused_computation.1 | loop fusion | bytes 524296 | tf_op jit(solution)/shard_map/dynamic_slice | solution.py:386
  1.1 0.7 %collective-permute-start.1 = (bf16[2,16,2048]{2,1,0:T(8,128)(2,1)S(1)}, bf16[2,16,2048]{2,1,0:T(8,128)(2,1)S(1)}, u32[]{:S(2)}, u32[]{:S(2)}) collective-permute-start(bf16[2,16,2048]{2,1,0:T(8,128)(2,1)S(1)} %get-tuple-element.19), channel_id=1, source_target_pairs={{8,16},{16,8},{24,32},{32,24},{40,48},{48,40},{56,64},{64,56},{72,... | collective-permute-start | bytes 393224 | tf_op jit(solution)/shard_map/ppermute | solution.py:390
  1.8 4.6 %collective-permute-start = (bf16[2,16,2048]{2,1,0:T(8,128)(2,1)S(1)}, bf16[2,16,2048]{2,1,0:T(8,128)(2,1)S(1)}, u32[]{:S(2)}, u32[]{:S(2)}) collective-permute-start(bf16[2,16,2048]{2,1,0:T(8,128)(2,1)S(1)} %get-tuple-element.20), channel_id=1, source_target_pairs={{0,8},{8,0},{16,24},{24,16},{32,40},{40,32},{48,56},{56,48},{64,72... | collective-permute-start | bytes 393224 | tf_op jit(solution)/shard_map/ppermute | solution.py:389
  6.3 1.2 %copy.9.w1 = bf16[1728,64]{1,0:T(8,128)(2,1)S(1)} copy(bf16[1728,64]{0,1:T(8,128)(2,1)} %param.12) | data formatting | bytes 442368 | tf_op args[4]
  7.5 1.2 %copy.10.w2 = bf16[1728,64]{1,0:T(8,128)(2,1)S(1)} copy(bf16[1728,64]{0,1:T(8,128)(2,1)} %param.13) | data formatting | bytes 442368 | tf_op args[5]
  8.8 0.0 copy-done.3
  8.8 0.0 copy-done.5
  8.8 0.0 copy-done.1
  8.8 1.5 %prepare.1 = (bf16[3,1152,256]{2,1,0:T(8,128)(2,1)S(1)}, bf16[3,1152,256]{2,1,0:T(8,128)(2,1)S(1)}, bf16[1024,1024]{1,0:T(8,128)(2,1)S(1)}, bf16[1024,256]{1,0:T(8,128)(2,1)S(1)}, bf16[256,128]{1,0:T(8,128)(2,1)S(1)}) custom-call(s32[8,16,32]{2,1,0:T(8,128)S(1)} %copy-done.1, s32[1,256]{1,0:T(1,128)S(1)} %copy-done.5, s32[64,128]{1,0:T(8,128)S(1)} %bitcast.7, ...), custom_call_target="tpu_custom_call" | custom-call | flops 100000000 | bytes 8388608 | tf_op jit(solution)/shard_map/prepare/pallas_call | solution.py:103
  10.2 0.1 pad_add_fusion.where
  10.3 0.0 collective-permute-done.1.xb
  10.3 0.0 collective-permute-done.xa
  10.3 0.0 copy-done
  10.3 0.8 %columns.1 = (bf16[32,2048]{1,0:T(8,128)(2,1)S(1)}, bf16[32,2048]{1,0:T(8,128)(2,1)S(1)}) custom-call(s32[4]{0:T(128)S(1)} %pad_add_fusion.where, bf16[8,16,2048]{2,1,0:T(8,128)(2,1)S(1)} %copy-done, bf16[2,16,2048]{2,1,0:T(8,128)(2,1)S(1)} %collective-permute-done.xa, bf16[2,16,2048]{2,1,0:T(8,128)(2,1)S(1)} %collective-permute-done.1.xb), custom_call_target="tpu_custom_call" | custom-call | tf_op jit(solution)/shard_map/columns/pallas_call | solution.py:155
  11.2 1.3 %collective-permute-start.2 = (bf16[32,2048]{1,0:T(8,128)(2,1)S(1)}, bf16[32,2048]{1,0:T(8,128)(2,1)S(1)}, u32[]{:S(2)}, u32[]{:S(2)}) collective-permute-start(bf16[32,2048]{1,0:T(8,128)(2,1)S(1)} %get-tuple-element.13.near), channel_id=1, source_target_pairs={{0,1},{1,0},{2,3},{3,2},{4,5},{5,4},{6,7},{7,6},{8,9},{9,8},{10,11... | collective-permute-start | bytes 393224 | tf_op jit(solution)/shard_map/ppermute | solution.py:395
  12.5 3.4 %collective-permute-start.3 = (bf16[32,2048]{1,0:T(8,128)(2,1)S(1)}, bf16[32,2048]{1,0:T(8,128)(2,1)S(1)}, u32[]{:S(2)}, u32[]{:S(2)}) collective-permute-start(bf16[32,2048]{1,0:T(8,128)(2,1)S(1)} %get-tuple-element.14.far), channel_id=1, source_target_pairs={{1,2},{2,1},{3,4},{4,3},{5,6},{6,5},{9,10},{10,9},{11,12},{12,11},... | collective-permute-start | bytes 393224 | tf_op jit(solution)/shard_map/ppermute | solution.py:396
  16.0 3.3 %inner.1.part = f32[1280,256]{1,0:T(8,128)S(1)} custom-call(s32[4]{0:T(128)S(1)} %pad_add_fusion.where, bf16[8,16,2048]{2,1,0:T(8,128)(2,1)S(1)} %copy-done, bf16[2,16,2048]{2,1,0:T(8,128)(2,1)S(1)} %collective-permute-done.xa, bf16[2,16,2048]{2,1,0:T(8,128)(2,1)S(1)} %collective-permute-done.1.xb, bf16[3,1152,256]{2,1,0:T(8,128)(2,1)S(1)} %get-tuple-element.12.wb.wb1), custom_call_target="tpu_custom_call" | custom-call | flops 4000000000 | bytes 2097152 | tf_op jit(solution)/shard_map/inner/pallas_call | solution.py:207
  19.3 0.0 collective-permute-done.2.ya
  19.3 0.0 collective-permute-done.3.yb
  19.3 0.0 copy-start.2
  19.3 0.0 copy-start.4
  19.4 7.4 %outer.1 = bf16[1024,128]{1,0:T(8,128)(2,1)S(1)} custom-call(s32[4]{0:T(128)S(1)} %pad_add_fusion.where, f32[1280,256]{1,0:T(8,128)S(1)} %inner.1.part, bf16[32,2048]{1,0:T(8,128)(2,1)S(1)} %get-tuple-element.13.near, bf16[32,2048]{1,0:T(8,128)(2,1)S(1)} %get-tuple-element.14.far, bf16[32,2048]{1,0:T(8,128)(2,1)S(1)} %collective-permute-done.2.ya, ...), custom_call_target="tpu_custom_call" | custom-call | tf_op jit(solution)/shard_map/outer/pallas_call | solution.py:330
  26.8 20.4 %all_to_all.5 = bf16[128,8,128]{2,1,0:T(8,128)(2,1)S(1)} all-to-all(bf16[128,8,128]{2,1,0:T(8,128)(2,1)S(1)} %bitcast.5), channel_id=1, replica_groups=mesh['gx'=16,'gy'=8] {'gx','gy'}, dimensions={0} | all-to-all | bytes 524288 | tf_op jit(solution)/shard_map/all_to_all | solution.py:400
  47.2 0.0 copy-done.2
  47.2 0.0 copy-done.4
  47.2 1.2 %head.1 = bf16[64,128]{1,0:T(8,128)(2,1)} custom-call(bf16[1024,128]{1,0:T(8,128)(2,1)S(1)} %bitcast.6, bf16[64,256]{1,0:T(8,128)(2,1)S(1)} %copy-done.4, bf16[256,128]{1,0:T(8,128)(2,1)S(1)} %copy-done.2), custom_call_target="tpu_custom_call" | custom-call | tf_op jit(solution)/shard_map/head/pallas_call | solution.py:363
Async XLA Ops:
  0.0 10.3 %copy-start = (bf16[8,16,2048]{2,1,0:T(8,128)(2,1)S(1)}, bf16[8,16,2048]{2,1,0:T(8,128)(2,1)}, u32[]{:S(2)}) copy-start(bf16[8,16,2048]{2,1,0:T(8,128)(2,1)} %v.3) | copy-start | bytes 1572868
  0.0 8.7 %copy-start.3 = (s32[8192]{0:T(1024)S(1)}, s32[8192]{0:T(1024)}, u32[]{:S(2)}) copy-start(s32[8192]{0:T(1024)} %param.11) | copy-start | bytes 98308
  0.0 8.8 %copy-start.5 = (s32[1,256]{1,0:T(1,128)S(1)}, s32[1,256]{1,0:T(1,128)}, u32[]{:S(2)}) copy-start(s32[1,256]{1,0:T(1,128)} %lists.1) | copy-start | bytes 3076
  0.0 8.8 %copy-start.1 = (s32[8,16,32]{2,1,0:T(8,128)S(1)}, s32[8,16,32]{2,1,0:T(8,128)}, u32[]{:S(2)}) copy-start(s32[8,16,32]{2,1,0:T(8,128)} %labels.1) | copy-start | bytes 49156
  1.1 9.2 %collective-permute-start.1 = (bf16[2,16,2048]{2,1,0:T(8,128)(2,1)S(1)}, bf16[2,16,2048]{2,1,0:T(8,128)(2,1)S(1)}, u32[]{:S(2)}, u32[]{:S(2)}) collective-permute-start(bf16[2,16,2048]{2,1,0:T(8,128)(2,1)S(1)} %get-tuple-element.19), channel_id=1, source_target_pairs={{8,16},{16,8},{24,32},{32,24},{40,48},{48,40},{56,64},{64,56},{72,... | collective-permute-start | bytes 393224 | tf_op jit(solution)/shard_map/ppermute | solution.py:390
  1.8 8.6 %collective-permute-start = (bf16[2,16,2048]{2,1,0:T(8,128)(2,1)S(1)}, bf16[2,16,2048]{2,1,0:T(8,128)(2,1)S(1)}, u32[]{:S(2)}, u32[]{:S(2)}) collective-permute-start(bf16[2,16,2048]{2,1,0:T(8,128)(2,1)S(1)} %get-tuple-element.20), channel_id=1, source_target_pairs={{0,8},{8,0},{16,24},{24,16},{32,40},{40,32},{48,56},{56,48},{64,72... | collective-permute-start | bytes 393224 | tf_op jit(solution)/shard_map/ppermute | solution.py:389
  11.2 8.1 %collective-permute-start.2 = (bf16[32,2048]{1,0:T(8,128)(2,1)S(1)}, bf16[32,2048]{1,0:T(8,128)(2,1)S(1)}, u32[]{:S(2)}, u32[]{:S(2)}) collective-permute-start(bf16[32,2048]{1,0:T(8,128)(2,1)S(1)} %get-tuple-element.13.near), channel_id=1, source_target_pairs={{0,1},{1,0},{2,3},{3,2},{4,5},{5,4},{6,7},{7,6},{8,9},{9,8},{10,11... | collective-permute-start | bytes 393224 | tf_op jit(solution)/shard_map/ppermute | solution.py:395
  12.5 6.8 %collective-permute-start.3 = (bf16[32,2048]{1,0:T(8,128)(2,1)S(1)}, bf16[32,2048]{1,0:T(8,128)(2,1)S(1)}, u32[]{:S(2)}, u32[]{:S(2)}) collective-permute-start(bf16[32,2048]{1,0:T(8,128)(2,1)S(1)} %get-tuple-element.14.far), channel_id=1, source_target_pairs={{1,2},{2,1},{3,4},{4,3},{5,6},{6,5},{9,10},{10,9},{11,12},{12,11},... | collective-permute-start | bytes 393224 | tf_op jit(solution)/shard_map/ppermute | solution.py:396
  19.3 27.9 %copy-start.2 = (bf16[256,128]{1,0:T(8,128)(2,1)S(1)}, bf16[256,128]{1,0:T(8,128)(2,1)}, u32[]{:S(2)}) copy-start(bf16[256,128]{1,0:T(8,128)(2,1)} %w_out.1) | copy-start | bytes 196612
  19.3 27.8 %copy-start.4 = (bf16[64,256]{1,0:T(8,128)(2,1)S(1)}, bf16[64,256]{1,0:T(8,128)(2,1)}, u32[]{:S(2)}) copy-start(bf16[64,256]{1,0:T(8,128)(2,1)} %w_in.1) | copy-start | bytes 98308

commit v2 on v1

v2 whole, which is shorter than its diff:
```python
import functools

import jax
import jax.numpy as jnp
from jax import lax
from jax.experimental import pallas as pl
from jax.experimental.pallas import tpu as pltpu
from jax.sharding import PartitionSpec as P

F32 = jnp.float32
BF16 = jnp.bfloat16
SX, SY, SZ, CH = 8, 16, 32, 64
LANES = SZ * CH
WIDE = LANES + 2 * CH
NB = 8
EX = SX + 4
FX = SX + 2
CAP = 8
STEP = 8
VMEM = pl.BlockSpec(memory_space=pltpu.VMEM)
SMEM = pl.BlockSpec(memory_space=pltpu.SMEM)


def params(mb=20):
    return pltpu.CompilerParams(vmem_limit_bytes=mb * 2**20)


def iota(shape, dim):
    return lax.broadcasted_iota(jnp.int32, shape, dim)


def dot(a, b):
    return jnp.dot(a, b, preferred_element_type=F32)


def widen(rows):
    zero = jnp.zeros((rows.shape[0], CH), rows.dtype)
    return jnp.concatenate([zero, rows, zero], axis=1)


def relu(rows):
    return jnp.maximum(rows, jnp.zeros_like(rows))


def begin_kernel(out):
    out[...] = jnp.zeros_like(out)


def begin():
    return pl.pallas_call(
        begin_kernel,
        out_shape=jax.ShapeDtypeStruct((8, 128), F32),
        out_specs=VMEM,
        cost_estimate=pl.CostEstimate(flops=10**10, bytes_accessed=4096, transcendentals=0),
        name="begin",
    )()


def band(wt_ref, out_ref):
    weight = wt_ref[...].astype(F32).T.astype(BF16)
    zero = jnp.zeros((CH, CH), BF16)
    quiet = jnp.zeros((128, 128), BF16)
    for kx in range(3):
        for ky in range(3):
            start = (kx * 3 + ky) * 3 * CH
            w = weight[start : start + 3 * CH, :]
            both = jnp.concatenate(
                [jnp.concatenate([w, zero], axis=0), jnp.concatenate([zero, w], axis=0)], axis=1
            )
            base = (ky * 3 + kx) * 384
            out_ref[base : base + 256, 0:128] = both
            out_ref[base + 128 : base + 384, 128:256] = both
            out_ref[base + 256 : base + 384, 0:128] = quiet
            out_ref[base : base + 128, 128:256] = quiet


def blocks(rows):
    return jnp.concatenate([rows[:, 256 * b : 256 * b + 256] for b in range(NB)], axis=0)


def unblocks(stack):
    n = stack.shape[0] // NB
    return jnp.concatenate([stack[n * b : n * b + n] for b in range(NB)], axis=1)


def shifts_y(wide):
    n = wide.shape[0]
    grid = wide.reshape(n // SY, SY, WIDE)
    zero = jnp.zeros((n // SY, 1, WIDE), wide.dtype)
    below = jnp.concatenate([zero, grid[:, : SY - 1]], axis=1).reshape(n, WIDE)
    above = jnp.concatenate([grid[:, 1:], zero], axis=1).reshape(n, WIDE)
    return below, wide, above


def windows(shifted, starts, rows):
    parts = []
    for b in range(NB):
        for start in starts:
            parts.append(
                jnp.concatenate(
                    [
                        ref[start + kx * SY : start + kx * SY + rows, 256 * b : 256 * b + 384]
                        for ref in shifted
                        for kx in range(3)
                    ],
                    axis=1,
                )
            )
    return jnp.concatenate(parts, axis=0)


def before_kernel(begun, v, labels, lists, home, w1t, w2t, wb1, wb2, member, place, meta, core, s0, s1, s2):
    slots = lists.shape[1]
    band(w1t, wb1)
    own = v[...].reshape(SX * SY, LANES)
    s0[...], s1[...], s2[...] = shifts_y(widen(relu(own)))
    conv = dot(windows((s0, s1, s2), (0,), (SX - 2) * SY), wb1[...])
    core[...] = (conv + blocks(own[SY : SX * SY - SY]).astype(F32)).astype(BF16)
    band(w2t, wb2)
    lab = labels[...].reshape(SX * SY, SZ).T
    ids = iota((slots, SX * SY), 0)
    count = jnp.zeros((slots, SX * SY), F32)
    for z in range(SZ):
        hit = jnp.broadcast_to(lab[z : z + 1, :], (slots, SX * SY)) == ids
        hot = hit.astype(F32)
        count = count + hot
        odd, half, b = z % 2, z // 2 % 2, z // 4
        at = b * 256 + half * 128
        member[odd * slots : (odd + 1) * slots, at : at + 128] = hot.astype(BF16)
    count = jnp.sum(count, axis=1, keepdims=True)
    li = lists[...]
    rows = home.shape[0]
    which = (iota((rows, slots), 0) == jnp.broadcast_to(li >> 7, (rows, slots))).astype(BF16)
    table = home[...]
    high = (table >> 6).astype(F32).T.astype(BF16)
    low = (table & 63).astype(F32).T.astype(BF16)
    lane = iota((128, slots), 0) == jnp.broadcast_to(li & 127, (128, slots))
    owner = jnp.sum(jnp.where(lane, dot(high, which), 0.0), axis=0, keepdims=True)
    row = jnp.sum(jnp.where(lane, dot(low, which), 0.0), axis=0, keepdims=True)
    across = jnp.broadcast_to(owner, (slots, slots))
    same = (across.T == across) & (iota((slots, slots), 0) < iota((slots, slots), 1))
    rank = jnp.sum(same.astype(F32), axis=0, keepdims=True)
    at = (owner * CAP + rank).astype(jnp.int32)
    total = place.shape[0]
    place[...] = (
        (iota((total, slots), 0) == jnp.broadcast_to(at, (total, slots))).astype(F32).astype(BF16)
    )
    key = jnp.broadcast_to(row + 1.0, (128, slots)).T
    count = jnp.broadcast_to(count, (slots, 128))
    big = jnp.floor(count * (1.0 / 64.0))
    lanes = iota((slots, 128), 1)
    info = jnp.where(lanes == 64, key, 0.0)
    info = jnp.where(lanes == 65, big, info)
    info = jnp.where(lanes == 66, count - 64.0 * big, info)
    meta[...] = info.astype(BF16)


def before(begun, v, labels, lists, home, w1t, w2t, devices):
    slots = lists.shape[1]
    return pl.pallas_call(
        before_kernel,
        out_shape=(
            jax.ShapeDtypeStruct((3456, 256), BF16),
            jax.ShapeDtypeStruct((3456, 256), BF16),
            jax.ShapeDtypeStruct((2 * slots, 2 * NB * SX * SY), BF16),
            jax.ShapeDtypeStruct((devices * CAP, slots), BF16),
            jax.ShapeDtypeStruct((slots, 128), BF16),
            jax.ShapeDtypeStruct((NB * (SX - 2) * SY, 256), BF16),
        ),
        in_specs=[VMEM] * 7,
        out_specs=(VMEM,) * 6,
        scratch_shapes=[pltpu.VMEM((SX * SY, WIDE), BF16)] * 3,
        compiler_params=params(),
        cost_estimate=pl.CostEstimate(flops=10**8, bytes_accessed=8 * 2**20, transcendentals=0),
        name="before",
    )(begun, v, labels, lists, home, w1t, w2t)


def choose(flag, yes, no):
    return jnp.where(flag, yes.astype(F32), no.astype(F32)).astype(BF16)


def x_extended(even, v, xa, xb):
    a = xa[...]
    b = xb[...]
    low = choose(even, b, a)
    high = choose(even, a, b)
    return jnp.concatenate([low, v[...], high], axis=0)


def columns_kernel(where, v, xa, xb, near, far):
    x_even = where[0] % 2 == 0
    y_even = where[1] % 2 == 0
    block = x_extended(x_even, v, xa, xb).reshape(EX * SY, LANES)
    r = iota((64, EX * SY), 0)
    c = r // 16
    y = jnp.where(c < 2, c, c + 12)
    pick = ((r % 16) * 16 + y == iota((64, EX * SY), 1)).astype(F32).astype(BF16)
    cols = dot(pick, block).astype(BF16)

    @pl.when(y_even)
    def _():
        near[...] = cols[32:64]
        far[...] = cols[0:32]

    @pl.when(jnp.logical_not(y_even))
    def _():
        near[...] = cols[0:32]
        far[...] = cols[32:64]


def columns(where, v, xa, xb):
    shape = jax.ShapeDtypeStruct((32, LANES), BF16)
    return pl.pallas_call(
        columns_kernel,
        out_shape=(shape, shape),
        in_specs=[SMEM, VMEM, VMEM, VMEM],
        out_specs=(VMEM, VMEM),
        compiler_params=params(),
        name="columns",
    )(where, v, xa, xb)


def slabs_kernel(where, v, xa, xb, core, near, far, wb, a0, a1, a2, own, cols, s0, s1, s2):
    gx, last_x = where[0], where[2] - 1
    x_even, y_even = where[0] % 2 == 0, where[1] % 2 == 0
    a, b = xa[...], xb[...]
    block = jnp.concatenate(
        [choose(x_even, b, a), v[0:2], v[SX - 2 : SX], choose(x_even, a, b)], axis=0
    ).reshape(8 * SY, LANES)
    s0[...], s1[...], s2[...] = shifts_y(widen(relu(block)))
    conv = dot(windows((s0, s1, s2), (0, 4 * SY), 2 * SY), wb[...])
    residual = jnp.concatenate([block[SY : 3 * SY], block[5 * SY : 7 * SY]], axis=0)
    x = iota((NB * 4 * SY, 256), 0) // SY % 4
    inside = ((x > 0) | (gx > 0)) & ((x < 3) | (gx < last_x))
    sides = jnp.where(inside, conv + blocks(residual).astype(F32), 0.0).astype(BF16)
    sides = unblocks(sides)
    main = jnp.concatenate([sides[0 : 2 * SY], unblocks(core[...]), sides[2 * SY :]], axis=0)
    own[...] = main[SY : SY + SX * SY]
    a0[...], a1[...], a2[...] = shifts_y(widen(relu(main)))
    low = choose(y_even, far[...], near[...])
    high = choose(y_even, near[...], far[...])
    side = relu(jnp.concatenate([low, high], axis=0))
    store_rolled(cols, widen(side))


def store_rolled(ref, wide):
    n = wide.shape[0]
    ref[0] = wide
    for kx in (1, 2):
        ref[kx] = pltpu.roll(wide, n - kx, 0)


def slabs(where, v, xa, xb, core, near, far, wb):
    full = jax.ShapeDtypeStruct((FX * SY, WIDE), BF16)
    return pl.pallas_call(
        slabs_kernel,
        out_shape=(
            full,
            full,
            full,
            jax.ShapeDtypeStruct((SX * SY, LANES), BF16),
            jax.ShapeDtypeStruct((3, 64, WIDE), BF16),
        ),
        in_specs=[SMEM] + [VMEM] * 7,
        out_specs=(VMEM,) * 5,
        scratch_shapes=[pltpu.VMEM((8 * SY, WIDE), BF16)] * 3,
        compiler_params=params(),
        cost_estimate=pl.CostEstimate(flops=2 * 10**9, bytes_accessed=2**20, transcendentals=0),
        name="slabs",
    )(where, v, xa, xb, core, near, far, wb)


def outer_kernel(
    where, a0i, a1i, a2i, owni, cols, near, far, ya, yb, wb1, a0, a1, a2, own, halo
):
    gx, gy = where[0], where[1]
    last_x, last_y = where[2] - 1, where[3] - 1
    y_even = gy % 2 == 0
    low = choose(y_even, yb[...], ya[...])
    high = choose(y_even, ya[...], yb[...])
    own_low = choose(y_even, far[...], near[...])
    own_high = choose(y_even, near[...], far[...])
    store_rolled(halo, widen(relu(jnp.concatenate([low, high], axis=0))))
    at = [(halo, 0), (halo, 16), (cols, 0), (cols, 16), (cols, 32), (cols, 48), (halo, 32), (halo, 48)]

    def group(g, kx, b):
        ref, start = at[g]
        return ref[kx, start : start + 16, 256 * b : 256 * b + 384]

    left = jnp.concatenate(
        [
            jnp.concatenate(
                [group(g + ky, kx, b) for ky in range(3) for kx in range(3)], axis=1
            )
            for b in range(NB)
            for g in (0, 1, 4, 5)
        ],
        axis=0,
    )
    conv = dot(left, wb1[...])
    residual = jnp.concatenate([low[16:32], own_low[0:16], own_high[16:32], high[0:16]], axis=0)
    residual = pltpu.roll(residual, 63, 0)
    row = iota((NB * 64, 256), 0)
    x = row % 16
    g = row // 16 % 4
    inside = ((x > 0) | (gx > 0)) & ((x < FX - 1) | (gx < last_x))
    inside = inside & ((g > 0) | (gy > 0)) & ((g < 3) | (gy < last_y))
    edge = jnp.where(inside, conv + blocks(residual).astype(F32), 0.0).astype(BF16)
    edge = unblocks(edge)
    wide = widen(relu(edge))
    for x in range(FX):
        s = SY * x
        a0[s : s + 1] = wide[x : x + 1]
        a0[s + 1 : s + 2] = wide[16 + x : 17 + x]
        a1[s : s + 1] = wide[16 + x : 17 + x]
        a1[s + SY - 1 : s + SY] = wide[32 + x : 33 + x]
        a2[s + SY - 2 : s + SY - 1] = wide[32 + x : 33 + x]
        a2[s + SY - 1 : s + SY] = wide[48 + x : 49 + x]
    for x in range(SX):
        s = SY * x
        own[s : s + 1] = edge[17 + x : 18 + x]
        own[s + SY - 1 : s + SY] = edge[33 + x : 34 + x]


def outer(where, a0, a1, a2, own, cols, near, far, ya, yb, wb1, wb2, member, place, meta):
    full = jax.ShapeDtypeStruct(a0.shape, BF16)
    a0, a1, a2, own = pl.pallas_call(
        outer_kernel,
        out_shape=(full, full, full, jax.ShapeDtypeStruct(own.shape, BF16)),
        in_specs=[SMEM] + [VMEM] * 10,
        out_specs=(VMEM,) * 4,
        scratch_shapes=[pltpu.VMEM((3, 64, WIDE), BF16)],
        input_output_aliases={1: 0, 2: 1, 3: 2, 4: 3},
        compiler_params=params(),
        name="outer",
    )(where, a0, a1, a2, own, cols, near, far, ya, yb, wb1)
    return pl.pallas_call(
        second_kernel,
        out_shape=jax.ShapeDtypeStruct((place.shape[0], 128), BF16),
        in_specs=[VMEM] * 8,
        out_specs=VMEM,
        scratch_shapes=[
            pltpu.VMEM((2 * meta.shape[0], 128), F32),
            pltpu.VMEM((256 * STEP, 128), BF16),
        ],
        compiler_params=params(),
        name="second",
    )(a0, a1, a2, own, wb2, member, place, meta)


def second_kernel(a0, a1, a2, own, wb2, member, place, meta, out, both, fresh):
    slots = meta.shape[0]
    both[...] = jnp.zeros_like(both)

    def block(i, carry):
        first = i * STEP
        left = jnp.concatenate(
            [
                jnp.concatenate(
                    [
                        ref[kx * SY : kx * SY + SX * SY, pl.ds(pl.multiple_of(256 * (first + b), 256), 384)]
                        for ref in (a0, a1, a2)
                        for kx in range(3)
                    ],
                    axis=1,
                )
                for b in range(STEP)
            ],
            axis=0,
        )
        conv = dot(left, wb2[...])
        for b in range(STEP):
            at = pl.multiple_of(256 * (first + b), 256)
            second = conv[128 * b : 128 * b + 128] + own[:, pl.ds(at, 256)].astype(F32)
            fresh[256 * b : 256 * b + 128] = second[:, 0:128].astype(BF16)
            fresh[256 * b + 128 : 256 * b + 256] = second[:, 128:256].astype(BF16)
        both[...] += dot(member[:, pl.ds(pl.multiple_of(256 * first, 256), 256 * STEP)], fresh[...])
        return carry

    lax.fori_loop(0, NB // STEP, block, 0)
    lanes = iota((slots, 128), 1)
    sums = both[0:slots] + pltpu.roll(both[slots : 2 * slots], 64, 1)
    rows = jnp.where(lanes < CH, sums, meta[...].astype(F32)).astype(BF16)
    out[...] = dot(place[...], rows).astype(BF16)


def head_kernel(got, w_in, w_out, out):
    rows = got[...]
    n = rows.shape[0]
    seg = out.shape[0]
    unit = (iota((8, 128), 1) == CH).astype(F32).astype(BF16)
    key = lax.dot_general(unit, rows, (((1,), (1,)), ((), ())), preferred_element_type=F32)
    key = jnp.broadcast_to(key[0:1], (seg, n))
    hit = (key == (iota((seg, n), 0) + 1).astype(F32)).astype(F32).astype(BF16)
    total = dot(hit, rows)
    lanes = iota((seg, 128), 1)
    digits = jnp.where(lanes == CH + 1, total * 64.0, jnp.where(lanes == CH + 2, total, 0.0))
    count = jnp.sum(digits, axis=1, keepdims=True)
    means = (total[:, 0:CH] / jnp.maximum(count, 1.0)).astype(BF16)
    hidden = jnp.maximum(dot(means, w_in[...]), 0.0).astype(BF16)
    out[...] = dot(hidden, w_out[...]).astype(BF16)


def head(got, w_in, w_out, seg):
    return pl.pallas_call(
        head_kernel,
        out_shape=jax.ShapeDtypeStruct((seg, w_out.shape[1]), BF16),
        in_specs=[VMEM] * 3,
        out_specs=VMEM,
        compiler_params=params(),
        name="head",
    )(got, w_in, w_out)


def pairs(count):
    inner_pairs = [(i, i ^ 1) for i in range(count)]
    outer_pairs = [(i, i + 1 if i % 2 else i - 1) for i in range(1, count - 1)]
    return inner_pairs, outer_pairs


def local(n_gx, n_gy, features, labels, lists, home, conv_first, conv_second, head_in, head_out):
    gx = lax.axis_index("gx")
    gy = lax.axis_index("gy")
    devices = n_gx * n_gy
    where = jnp.stack([gx, gy, jnp.int32(n_gx), jnp.int32(n_gy)]).astype(jnp.int32)
    even = gx % 2 == 0
    to_a = lax.dynamic_slice_in_dim(features, jnp.where(even, SX - 2, 0), 2, 0)
    to_b = lax.dynamic_slice_in_dim(features, jnp.where(even, 0, SX - 2), 2, 0)
    inner_x, outer_x = pairs(n_gx)
    inner_y, outer_y = pairs(n_gy)
    xa = lax.ppermute(to_a, "gx", inner_x)
    xb = lax.ppermute(to_b, "gx", outer_x)
    wb1, wb2, member, place, meta, core = before(
        begin(), features, labels, lists, home.reshape(-1, 128), conv_first.T, conv_second.T, devices
    )
    near, far = columns(where, features, xa, xb)
    ya = lax.ppermute(near, "gy", inner_y)
    yb = lax.ppermute(far, "gy", outer_y)
    a0, a1, a2, own, cols = slabs(where, features, xa, xb, core, near, far, wb1)
    rows = outer(where, a0, a1, a2, own, cols, near, far, ya, yb, wb1, wb2, member, place, meta)
    rows = rows.reshape(devices, CAP, 128)
    got = lax.all_to_all(rows, ("gx", "gy"), 0, 0, tiled=True)
    return head(got.reshape(devices * CAP, 128), head_in, head_out, home.size // devices)


def solution(mesh):
    placed = (
        P("gx", "gy", None),
        P("gx", "gy", None),
        P(("gx", "gy"), None),
        P(),
        P(),
        P(),
        P(),
        P(),
    )
    return jax.shard_map(
        functools.partial(local, mesh.shape["gx"], mesh.shape["gy"]),
        mesh=mesh,
        in_specs=placed,
        out_specs=P(("gx", "gy"), None),
        check_vma=False,
    )
```

time: 48.7 us -> 47.1 us (0.967)
  local copies, waits for them, and re-layouts: 3.49 us -> 1.72 us
  waiting for transfers between devices: 0.01 us -> 0.72 us
    unnamed x14 -> x18, local copies, waits for them, and re-layouts: 2.44 us -> 0.73 us
    ppermute x1, waiting for transfers between devices: 0.01 us -> 0.71 us  [local(): yb = lax.ppermute(far, 'gy', outer_y)]
    pallas_call x3 -> x5, Pallas kernels: 12.3 us -> 12 us  [the longest x1 4.19 us: outer(): pl.pallas_call(second_kernel, out_shape=jax.ShapeDtypeStruct((place.shape...]
  transfers between devices with their start and end apart: 4 -> 4, of which waited for: 0 -> 1; matrix products, arithmetic and copies ran while one was open for 5% -> 0% of each run, Pallas kernels for 10% -> 12%
where the time goes in v2:
time: 47.1 us; the launch traced here: 46.9 us
  blocking collectives  20.2 us (43%)
  Pallas kernels  14.1 us (30%)
  starting transfers between devices  10 us (21%)
  local copies, waits for them, and re-layouts  1.72 us (4%)
  waiting for transfers between devices  0.72 us (2%)
    all_to_all x1, blocking collectives, local(): got = lax.all_to_all(rows, ('gx', 'gy'), 0, 0, tiled=True)  20.2 us
    ppermute x1, starting transfers between devices, local(): xa = lax.ppermute(to_a, 'gx', inner_x)  4.57 us
    pallas_call x1, Pallas kernels, outer(): pl.pallas_call(second_kernel, out_shape=jax.ShapeDtypeStruct((place.shape...  4.19 us
    ppermute x1, starting transfers between devices, local(): yb = lax.ppermute(far, 'gy', outer_y)  3.44 us
    pallas_call x1, Pallas kernels, before(): pl.pallas_call(before_kernel, out_shape=(jax.ShapeDtypeStruct((3456, 256)...  3.09 us
    pallas_call x1, Pallas kernels, slabs(): pl.pallas_call(slabs_kernel, out_shape=(full, full, full, jax.ShapeDtypeS...  2.09 us
    pallas_call x1, Pallas kernels, outer(): pl.pallas_call(outer_kernel, out_shape=(full, full, full, jax.ShapeDtypeS...  2.04 us
    ppermute x1, starting transfers between devices, local(): ya = lax.ppermute(near, 'gy', inner_y)  1.32 us
  transfers between devices with their start and end apart: 4, of which 1 were waited for; matrix products, arithmetic and copies ran while one was open for 0% of the time, Pallas kernels for 12%

profile of v2, /device:TPU:1, one launch (start us, length us, event | category | flops | bytes accessed | tf_op | source)
XLA Modules:
  0.0 46.9 jit_solution(14015572062259734978)
XLA Ops:
  0.0 1.0 %constant_dynamic-slice_fusion = (bf16[2,16,2048]{2,1,0:T(8,128)(2,1)S(1)}, bf16[2,16,2048]{2,1,0:T(8,128)(2,1)S(1)}) fusion(bf16[8,16,2048]{2,1,0:T(8,128)(2,1)} %v.5, s32[]{:T(128)S(6)} %select_n.18, s32[]{:T(128)S(6)} %select_n.17), kind=kLoop, calls=%fused_computation.1 | loop fusion | bytes 524296 | tf_op jit(solution)/shard_map/dynamic_slice | solution.py:429
  1.0 0.7 %collective-permute-start.1 = (bf16[2,16,2048]{2,1,0:T(8,128)(2,1)S(1)}, bf16[2,16,2048]{2,1,0:T(8,128)(2,1)S(1)}, u32[]{:S(2)}, u32[]{:S(2)}) collective-permute-start(bf16[2,16,2048]{2,1,0:T(8,128)(2,1)S(1)} %get-tuple-element.39), channel_id=1, source_target_pairs={{8,16},{16,8},{24,32},{32,24},{40,48},{48,40},{56,64},{64,56},{72,... | collective-permute-start | bytes 393224 | tf_op jit(solution)/shard_map/ppermute | solution.py:433
  1.7 0.0 copy-start
  1.7 0.0 copy-start.1
  1.7 0.0 copy-start.2
  1.7 0.0 copy-start.3
  1.7 0.0 copy-start.5
  1.7 0.0 copy-start.8
  1.7 4.6 %collective-permute-start = (bf16[2,16,2048]{2,1,0:T(8,128)(2,1)S(1)}, bf16[2,16,2048]{2,1,0:T(8,128)(2,1)S(1)}, u32[]{:S(2)}, u32[]{:S(2)}) collective-permute-start(bf16[2,16,2048]{2,1,0:T(8,128)(2,1)S(1)} %get-tuple-element.40), channel_id=1, source_target_pairs={{0,8},{8,0},{16,24},{24,16},{32,40},{40,32},{48,56},{56,48},{64,72... | collective-permute-start | bytes 393224 | tf_op jit(solution)/shard_map/ppermute | solution.py:432
  6.3 0.6 %begin.1.begun = f32[8,128]{1,0:T(8,128)} custom-call(), custom_call_target="tpu_custom_call" | custom-call | flops 10000000000 | bytes 4096 | tf_op jit(solution)/shard_map/begin/pallas_call | solution.py:50
  6.9 0.0 copy-done
  6.9 0.0 copy-done.1
  6.9 0.0 copy-done.2
  6.9 0.0 copy-done.3
  6.9 0.0 copy-done.5
  6.9 0.0 copy-done.8
  6.9 0.0 copy-start.7
  6.9 0.7 %copy-done.7 = f32[8,128]{1,0:T(8,128)S(1)} copy-done((f32[8,128]{1,0:T(8,128)S(1)}, f32[8,128]{1,0:T(8,128)}, u32[]{:S(2)}) %copy-start.7) | copy-done | bytes 4120
  7.6 3.1 %before.1 = (bf16[3456,256]{1,0:T(8,128)(2,1)S(1)}, bf16[3456,256]{1,0:T(8,128)(2,1)S(1)}, bf16[512,2048]{1,0:T(8,128)(2,1)S(1)}, bf16[1024,256]{1,0:T(8,128)(2,...) custom-call(f32[8,128]{1,0:T(8,128)S(1)} %copy-done.7, bf16[8,16,2048]{2,1,0:T(8,128)(2,1)S(1)} %copy-done, ...), custom_call_target="tpu_custom_call" | custom-call | flops 100000000 | bytes 8388608 | tf_op jit(solution)/shard_map/before/pallas_call | solution.py:160
  10.7 0.1 pad_add_fusion.where
  10.8 0.0 collective-permute-done.1.xb
  10.8 0.0 collective-permute-done.xa
  10.8 0.8 %columns.1 = (bf16[32,2048]{1,0:T(8,128)(2,1)S(1)}, bf16[32,2048]{1,0:T(8,128)(2,1)S(1)}) custom-call(s32[4]{0:T(128)S(1)} %pad_add_fusion.where, bf16[8,16,2048]{2,1,0:T(8,128)(2,1)S(1)} %copy-done, bf16[2,16,2048]{2,1,0:T(8,128)(2,1)S(1)} %collective-permute-done.xa, bf16[2,16,2048]{2,1,0:T(8,128)(2,1)S(1)} %collective-permute-done.1.xb), custom_call_target="tpu_custom_call" | custom-call | tf_op jit(solution)/shard_map/columns/pallas_call | solution.py:214
  11.7 1.3 %collective-permute-start.2 = (bf16[32,2048]{1,0:T(8,128)(2,1)S(1)}, bf16[32,2048]{1,0:T(8,128)(2,1)S(1)}, u32[]{:S(2)}, u32[]{:S(2)}) collective-permute-start(bf16[32,2048]{1,0:T(8,128)(2,1)S(1)} %get-tuple-element.23.near), channel_id=1, source_target_pairs={{0,1},{1,0},{2,3},{3,2},{4,5},{5,4},{6,7},{7,6},{8,9},{9,8},{10,11... | collective-permute-start | bytes 393224 | tf_op jit(solution)/shard_map/ppermute | solution.py:438
  13.0 3.4 %collective-permute-start.3 = (bf16[32,2048]{1,0:T(8,128)(2,1)S(1)}, bf16[32,2048]{1,0:T(8,128)(2,1)S(1)}, u32[]{:S(2)}, u32[]{:S(2)}) collective-permute-start(bf16[32,2048]{1,0:T(8,128)(2,1)S(1)} %get-tuple-element.24.far), channel_id=1, source_target_pairs={{1,2},{2,1},{3,4},{4,3},{5,6},{6,5},{9,10},{10,9},{11,12},{12,11},... | collective-permute-start | bytes 393224 | tf_op jit(solution)/shard_map/ppermute | solution.py:439
  16.4 2.1 %slabs.1 = (bf16[160,2176]{1,0:T(8,128)(2,1)S(1)}, bf16[160,2176]{1,0:T(8,128)(2,1)S(1)}, bf16[160,2176]{1,0:T(8,128)(2,1)S(1)}, bf16[128,2048]{1,0:T(8,128)(2,1)S(1)}, bf16[3,64,2176]{2,1,0:T(8,128)(2,1)S(1)}) custom-call(s32[4]{0:T(128)S(1)} %pad_add_fusion.where, bf16[8,16,2048]{2,1,0:T(8,128)(2,1)S(1)} %copy-done, ...), custom_call_target="tpu_custom_call" | custom-call | flops 2000000000 | bytes 1048576 | tf_op jit(solution)/shard_map/slabs/pallas_call | solution.py:256
  18.5 0.0 collective-permute-done.2.ya
  18.5 0.7 %collective-permute-done.3.yb = bf16[32,2048]{1,0:T(8,128)(2,1)S(1)} collective-permute-done((bf16[32,2048]{1,0:T(8,128)(2,1)S(1)}, bf16[32,2048]{1,0:T(8,128)(2,1)S(1)}, u32[]{:S(2)}, u32[]{:S(2)}) %collective-permute-start.3) | collective-permute-done | bytes 131104 | tf_op jit(solution)/shard_map/ppermute | solution.py:439
  19.3 2.0 %outer.1 = (bf16[160,2176]{1,0:T(8,128)(2,1)S(1)}, bf16[160,2176]{1,0:T(8,128)(2,1)S(1)}, bf16[160,2176]{1,0:T(8,128)(2,1)S(1)}, bf16[128,2048]{1,0:T(8,128)(2,1)S(1)}) custom-call(s32[4]{0:T(128)S(1)} %pad_add_fusion.where, bf16[160,2176]{1,0:T(8,128)(2,1)S(1)} %get-tuple-element.26.a0i, ...), custom_call_target="tpu_custom_call", output_to_operand_aliasing={{0}: (1, {}), {1}: (2, {}), {2}: (3, {}), {3}: (4, {})} | custom-call | tf_op jit(solution)/shard_map/outer/pallas_call | solution.py:328
  21.3 0.0 copy-start.4
  21.3 0.0 copy-start.6
  21.3 4.2 %second.1 = bf16[1024,128]{1,0:T(8,128)(2,1)S(1)} custom-call(bf16[160,2176]{1,0:T(8,128)(2,1)S(1)} %get-tuple-element.31.a0, bf16[160,2176]{1,0:T(8,128)(2,1)S(1)} %get-tuple-element.32.a1, bf16[160,2176]{1,0:T(8,128)(2,1)S(1)} %get-tuple-element.33.a2, bf16[128,2048]{1,0:T(8,128)(2,1)S(1)} %get-tuple-element.34.own, ...), custom_call_target="tpu_custom_call" | custom-call | tf_op jit(solution)/shard_map/second/pallas_call | solution.py:338
  25.5 20.2 %all_to_all.5 = bf16[128,8,128]{2,1,0:T(8,128)(2,1)S(1)} all-to-all(bf16[128,8,128]{2,1,0:T(8,128)(2,1)S(1)} %bitcast.7), channel_id=1, replica_groups=mesh['gx'=16,'gy'=8] {'gx','gy'}, dimensions={0} | all-to-all | bytes 524288 | tf_op jit(solution)/shard_map/all_to_all | solution.py:443
  45.7 0.0 copy-done.4
  45.7 0.0 copy-done.6
  45.7 1.2 %head.1 = bf16[64,128]{1,0:T(8,128)(2,1)} custom-call(bf16[1024,128]{1,0:T(8,128)(2,1)S(1)} %bitcast.8, bf16[64,256]{1,0:T(8,128)(2,1)S(1)} %copy-done.6, bf16[256,128]{1,0:T(8,128)(2,1)S(1)} %copy-done.4), custom_call_target="tpu_custom_call" | custom-call | tf_op jit(solution)/shard_map/head/pallas_call | solution.py:406
Async XLA Ops:
  1.0 9.8 %collective-permute-start.1 = (bf16[2,16,2048]{2,1,0:T(8,128)(2,1)S(1)}, bf16[2,16,2048]{2,1,0:T(8,128)(2,1)S(1)}, u32[]{:S(2)}, u32[]{:S(2)}) collective-permute-start(bf16[2,16,2048]{2,1,0:T(8,128)(2,1)S(1)} %get-tuple-element.39), channel_id=1, source_target_pairs={{8,16},{16,8},{24,32},{32,24},{40,48},{48,40},{56,64},{64,56},{72,... | collective-permute-start | bytes 393224 | tf_op jit(solution)/shard_map/ppermute | solution.py:433
  1.7 5.2 %copy-start = (bf16[8,16,2048]{2,1,0:T(8,128)(2,1)S(1)}, bf16[8,16,2048]{2,1,0:T(8,128)(2,1)}, u32[]{:S(2)}) copy-start(bf16[8,16,2048]{2,1,0:T(8,128)(2,1)} %v.5) | copy-start | bytes 1572868
  1.7 5.2 %copy-start.1 = (bf16[1728,64]{0,1:T(8,128)(2,1)S(1)}, bf16[1728,64]{0,1:T(8,128)(2,1)}, u32[]{:S(2)}) copy-start(bf16[1728,64]{0,1:T(8,128)(2,1)} %param.12) | copy-start | bytes 663556
  1.7 5.2 %copy-start.2 = (bf16[1728,64]{0,1:T(8,128)(2,1)S(1)}, bf16[1728,64]{0,1:T(8,128)(2,1)}, u32[]{:S(2)}) copy-start(bf16[1728,64]{0,1:T(8,128)(2,1)} %param.13) | copy-start | bytes 663556
  1.7 5.2 %copy-start.3 = (s32[8,16,32]{2,1,0:T(8,128)S(1)}, s32[8,16,32]{2,1,0:T(8,128)}, u32[]{:S(2)}) copy-start(s32[8,16,32]{2,1,0:T(8,128)} %labels.1) | copy-start | bytes 49156
  1.7 5.2 %copy-start.5 = (s32[8192]{0:T(1024)S(1)}, s32[8192]{0:T(1024)}, u32[]{:S(2)}) copy-start(s32[8192]{0:T(1024)} %param.11) | copy-start | bytes 98308
  1.7 5.2 %copy-start.8 = (s32[1,256]{1,0:T(1,128)S(1)}, s32[1,256]{1,0:T(1,128)}, u32[]{:S(2)}) copy-start(s32[1,256]{1,0:T(1,128)} %lists.1) | copy-start | bytes 3076
  1.7 9.1 %collective-permute-start = (bf16[2,16,2048]{2,1,0:T(8,128)(2,1)S(1)}, bf16[2,16,2048]{2,1,0:T(8,128)(2,1)S(1)}, u32[]{:S(2)}, u32[]{:S(2)}) collective-permute-start(bf16[2,16,2048]{2,1,0:T(8,128)(2,1)S(1)} %get-tuple-element.40), channel_id=1, source_target_pairs={{0,8},{8,0},{16,24},{24,16},{32,40},{40,32},{48,56},{56,48},{64,72... | collective-permute-start | bytes 393224 | tf_op jit(solution)/shard_map/ppermute | solution.py:432
  6.9 0.7 %copy-start.7 = (f32[8,128]{1,0:T(8,128)S(1)}, f32[8,128]{1,0:T(8,128)}, u32[]{:S(2)}) copy-start(f32[8,128]{1,0:T(8,128)} %begin.1.begun) | copy-start | bytes 12292
  11.7 6.9 %collective-permute-start.2 = (bf16[32,2048]{1,0:T(8,128)(2,1)S(1)}, bf16[32,2048]{1,0:T(8,128)(2,1)S(1)}, u32[]{:S(2)}, u32[]{:S(2)}) collective-permute-start(bf16[32,2048]{1,0:T(8,128)(2,1)S(1)} %get-tuple-element.23.near), channel_id=1, source_target_pairs={{0,1},{1,0},{2,3},{3,2},{4,5},{5,4},{6,7},{7,6},{8,9},{9,8},{10,11... | collective-permute-start | bytes 393224 | tf_op jit(solution)/shard_map/ppermute | solution.py:438
  13.0 6.3 %collective-permute-start.3 = (bf16[32,2048]{1,0:T(8,128)(2,1)S(1)}, bf16[32,2048]{1,0:T(8,128)(2,1)S(1)}, u32[]{:S(2)}, u32[]{:S(2)}) collective-permute-start(bf16[32,2048]{1,0:T(8,128)(2,1)S(1)} %get-tuple-element.24.far), channel_id=1, source_target_pairs={{1,2},{2,1},{3,4},{4,3},{5,6},{6,5},{9,10},{10,9},{11,12},{12,11},... | collective-permute-start | bytes 393224 | tf_op jit(solution)/shard_map/ppermute | solution.py:439
  21.3 24.4 %copy-start.4 = (bf16[256,128]{1,0:T(8,128)(2,1)S(1)}, bf16[256,128]{1,0:T(8,128)(2,1)}, u32[]{:S(2)}) copy-start(bf16[256,128]{1,0:T(8,128)(2,1)} %w_out.1) | copy-start | bytes 196612
  21.3 24.4 %copy-start.6 = (bf16[64,256]{1,0:T(8,128)(2,1)S(1)}, bf16[64,256]{1,0:T(8,128)(2,1)}, u32[]{:S(2)}) copy-start(bf16[64,256]{1,0:T(8,128)(2,1)} %w_in.1) | copy-start | bytes 98308

commit v3 on v2

--- a/solution.py
+++ b/solution.py
@@ -16,7 +16,6 @@
 EX = SX + 4
 FX = SX + 2
 CAP = 8
-STEP = 8
 VMEM = pl.BlockSpec(memory_space=pltpu.VMEM)
 SMEM = pl.BlockSpec(memory_space=pltpu.SMEM)
 
@@ -43,14 +42,14 @@
 
 
 def begin_kernel(out):
-    out[...] = jnp.zeros_like(out)
+    pass
 
 
 def begin():
     return pl.pallas_call(
         begin_kernel,
-        out_shape=jax.ShapeDtypeStruct((8, 128), F32),
-        out_specs=VMEM,
+        out_shape=jax.ShapeDtypeStruct((12 * 2**20,), F32),
+        out_specs=pl.BlockSpec(memory_space=pl.ANY),
         cost_estimate=pl.CostEstimate(flops=10**10, bytes_accessed=4096, transcendentals=0),
         name="begin",
     )()
@@ -167,7 +166,7 @@
             jax.ShapeDtypeStruct((slots, 128), BF16),
             jax.ShapeDtypeStruct((NB * (SX - 2) * SY, 256), BF16),
         ),
-        in_specs=[VMEM] * 7,
+        in_specs=[pl.BlockSpec(memory_space=pl.ANY)] + [VMEM] * 6,
         out_specs=(VMEM,) * 6,
         scratch_shapes=[pltpu.VMEM((SX * SY, WIDE), BF16)] * 3,
         compiler_params=params(),
@@ -188,7 +187,7 @@
     return jnp.concatenate([low, v[...], high], axis=0)
 
 
-def columns_kernel(where, v, xa, xb, near, far):
+def columns_kernel(where, v, xb, xa, near, far):
     x_even = where[0] % 2 == 0
     y_even = where[1] % 2 == 0
     block = x_extended(x_even, v, xa, xb).reshape(EX * SY, LANES)
@@ -218,10 +217,10 @@
         out_specs=(VMEM, VMEM),
         compiler_params=params(),
         name="columns",
-    )(where, v, xa, xb)
-
-
-def slabs_kernel(where, v, xa, xb, core, near, far, wb, a0, a1, a2, own, cols, s0, s1, s2):
+    )(where, v, xb, xa)
+
+
+def slabs_kernel(where, v, xb, xa, core, near, far, wb, a0, a1, a2, own, cols, s0, s1, s2):
     gx, last_x = where[0], where[2] - 1
     x_even, y_even = where[0] % 2 == 0, where[1] % 2 == 0
     a, b = xa[...], xb[...]
@@ -268,7 +267,7 @@
         compiler_params=params(),
         cost_estimate=pl.CostEstimate(flops=2 * 10**9, bytes_accessed=2**20, transcendentals=0),
         name="slabs",
-    )(where, v, xa, xb, core, near, far, wb)
+    )(where, v, xb, xa, core, near, far, wb)
 
 
 def outer_kernel(
@@ -340,45 +339,28 @@
         out_shape=jax.ShapeDtypeStruct((place.shape[0], 128), BF16),
         in_specs=[VMEM] * 8,
         out_specs=VMEM,
-        scratch_shapes=[
-            pltpu.VMEM((2 * meta.shape[0], 128), F32),
-            pltpu.VMEM((256 * STEP, 128), BF16),
-        ],
+        scratch_shapes=[pltpu.VMEM((256 * NB, 128), BF16)],
         compiler_params=params(),
         name="second",
     )(a0, a1, a2, own, wb2, member, place, meta)
 
 
-def second_kernel(a0, a1, a2, own, wb2, member, place, meta, out, both, fresh):
+def second_kernel(a0, a1, a2, own, wb2, member, place, meta, out, fresh):
     slots = meta.shape[0]
-    both[...] = jnp.zeros_like(both)
-
-    def block(i, carry):
-        first = i * STEP
+    for b in range(NB):
+        at = 256 * b
         left = jnp.concatenate(
             [
-                jnp.concatenate(
-                    [
-                        ref[kx * SY : kx * SY + SX * SY, pl.ds(pl.multiple_of(256 * (first + b), 256), 384)]
-                        for ref in (a0, a1, a2)
-                        for kx in range(3)
-                    ],
-                    axis=1,
-                )
-                for b in range(STEP)
+                ref[kx * SY : kx * SY + SX * SY, at : at + 384]
+                for ref in (a0, a1, a2)
+                for kx in range(3)
             ],
-            axis=0,
+            axis=1,
         )
-        conv = dot(left, wb2[...])
-        for b in range(STEP):
-            at = pl.multiple_of(256 * (first + b), 256)
-            second = conv[128 * b : 128 * b + 128] + own[:, pl.ds(at, 256)].astype(F32)
-            fresh[256 * b : 256 * b + 128] = second[:, 0:128].astype(BF16)
-            fresh[256 * b + 128 : 256 * b + 256] = second[:, 128:256].astype(BF16)
-        both[...] += dot(member[:, pl.ds(pl.multiple_of(256 * first, 256), 256 * STEP)], fresh[...])
-        return carry
-
-    lax.fori_loop(0, NB // STEP, block, 0)
+        second = dot(left, wb2[...]) + own[:, at : at + 256].astype(F32)
+        fresh[at : at + 128] = second[:, 0:128].astype(BF16)
+        fresh[at + 128 : at + 256] = second[:, 128:256].astype(BF16)
+    both = dot(member[...], fresh[...])
     lanes = iota((slots, 128), 1)
     sums = both[0:slots] + pltpu.roll(both[slots : 2 * slots], 64, 1)
     rows = jnp.where(lanes < CH, sums, meta[...].astype(F32)).astype(BF16)
@@ -429,14 +411,14 @@
     to_b = lax.dynamic_slice_in_dim(features, jnp.where(even, 0, SX - 2), 2, 0)
     inner_x, outer_x = pairs(n_gx)
     inner_y, outer_y = pairs(n_gy)
+    xb = lax.ppermute(to_b, "gx", outer_x)
     xa = lax.ppermute(to_a, "gx", inner_x)
-    xb = lax.ppermute(to_b, "gx", outer_x)
     wb1, wb2, member, place, meta, core = before(
         begin(), features, labels, lists, home.reshape(-1, 128), conv_first.T, conv_second.T, devices
     )
     near, far = columns(where, features, xa, xb)
+    yb = lax.ppermute(far, "gy", outer_y)
     ya = lax.ppermute(near, "gy", inner_y)
-    yb = lax.ppermute(far, "gy", outer_y)
     a0, a1, a2, own, cols = slabs(where, features, xa, xb, core, near, far, wb1)
     rows = outer(where, a0, a1, a2, own, cols, near, far, ya, yb, wb1, wb2, member, place, meta)
     rows = rows.reshape(devices, CAP, 128)

time: 47.1 us -> 46.2 us (0.981)
  Pallas kernels: 14.1 us -> 12.6 us
  blocking collectives: 20.2 us -> 21.4 us
  local copies, waits for them, and re-layouts: 1.72 us -> 1.04 us
    all_to_all x1, blocking collectives: 20.2 us -> 21.4 us  [local(): got = lax.all_to_all(rows, ('gx', 'gy'), 0, 0, tiled=True)]
    pallas_call x1, Pallas kernels: 4.19 us -> 3.25 us  [outer(): pl.pallas_call(second_kernel, out_shape=jax.ShapeDtypeStruct((place.shape...]
    unnamed x18 -> x16, local copies, waits for them, and re-layouts: 0.73 us -> 0.05 us
    pallas_call x1, Pallas kernels: 0.59 us -> 0.01 us  [begin(): pl.pallas_call(begin_kernel, out_shape=jax.ShapeDtypeStruct((12 * 2 ** 20...]
  transfers between devices with their start and end apart: 4 -> 4, of which waited for: 1 -> 1; matrix products, arithmetic and copies ran while one was open for 0% -> 0% of each run, Pallas kernels for 12% -> 11%
where the time goes in v3:
time: 46.2 us; the launch traced here: 46 us
  blocking collectives  21.4 us (46%)
  Pallas kernels  12.6 us (27%)
  starting transfers between devices  10 us (22%)
  local copies, waits for them, and re-layouts  1.04 us (2%)
  waiting for transfers between devices  0.72 us (2%)
    all_to_all x1, blocking collectives, local(): got = lax.all_to_all(rows, ('gx', 'gy'), 0, 0, tiled=True)  21.4 us
    ppermute x1, starting transfers between devices, local(): xa = lax.ppermute(to_a, 'gx', inner_x)  4.57 us
    ppermute x1, starting transfers between devices, local(): yb = lax.ppermute(far, 'gy', outer_y)  3.44 us
    pallas_call x1, Pallas kernels, outer(): pl.pallas_call(second_kernel, out_shape=jax.ShapeDtypeStruct((place.shape...  3.25 us
    pallas_call x1, Pallas kernels, before(): pl.pallas_call(before_kernel, out_shape=(jax.ShapeDtypeStruct((3456, 256)...  3.09 us
    pallas_call x1, Pallas kernels, slabs(): pl.pallas_call(slabs_kernel, out_shape=(full, full, full, jax.ShapeDtypeS...  2.1 us
    pallas_call x1, Pallas kernels, outer(): pl.pallas_call(outer_kernel, out_shape=(full, full, full, jax.ShapeDtypeS...  2.03 us
    ppermute x1, starting transfers between devices, local(): ya = lax.ppermute(near, 'gy', inner_y)  1.32 us
  transfers between devices with their start and end apart: 4, of which 1 were waited for; matrix products, arithmetic and copies ran while one was open for 0% of the time, Pallas kernels for 11%

profile of v3, /device:TPU:1, one launch (start us, length us, event | category | flops | bytes accessed | tf_op | source)
XLA Modules:
  0.0 46.0 jit_solution(14747930609600185621)
XLA Ops:
  0.0 1.0 %constant_dynamic-slice_fusion = (bf16[2,16,2048]{2,1,0:T(8,128)(2,1)S(1)}, bf16[2,16,2048]{2,1,0:T(8,128)(2,1)S(1)}) fusion(bf16[8,16,2048]{2,1,0:T(8,128)(2,1)} %v.5, s32[]{:T(128)S(6)} %select_n.18, s32[]{:T(128)S(6)} %select_n.17), kind=kLoop, calls=%fused_computation.1 | loop fusion | bytes 524296 | tf_op jit(solution)/shard_map/dynamic_slice | solution.py:410
  1.0 0.7 %collective-permute-start = (bf16[2,16,2048]{2,1,0:T(8,128)(2,1)S(1)}, bf16[2,16,2048]{2,1,0:T(8,128)(2,1)S(1)}, u32[]{:S(2)}, u32[]{:S(2)}) collective-permute-start(bf16[2,16,2048]{2,1,0:T(8,128)(2,1)S(1)} %get-tuple-element.40), channel_id=1, source_target_pairs={{8,16},{16,8},{24,32},{32,24},{40,48},{48,40},{56,64},{64,56},{72,... | collective-permute-start | bytes 393224 | tf_op jit(solution)/shard_map/ppermute | solution.py:414
  1.7 0.0 copy-start
  1.7 0.0 copy-start.1
  1.7 0.0 copy-start.2
  1.7 0.0 copy-start.3
  1.7 0.0 copy-start.5
  1.7 0.0 copy-start.7
  1.7 4.6 %collective-permute-start.1 = (bf16[2,16,2048]{2,1,0:T(8,128)(2,1)S(1)}, bf16[2,16,2048]{2,1,0:T(8,128)(2,1)S(1)}, u32[]{:S(2)}, u32[]{:S(2)}) collective-permute-start(bf16[2,16,2048]{2,1,0:T(8,128)(2,1)S(1)} %get-tuple-element.39), channel_id=1, source_target_pairs={{0,8},{8,0},{16,24},{24,16},{32,40},{40,32},{48,56},{56,48},{64,72... | collective-permute-start | bytes 393224 | tf_op jit(solution)/shard_map/ppermute | solution.py:415
  6.3 0.0 copy-done
  6.3 0.0 copy-done.1
  6.3 0.0 copy-done.2
  6.3 0.0 copy-done.3
  6.3 0.0 copy-done.5
  6.3 0.0 copy-done.7
  6.4 3.1 %before.1 = (bf16[3456,256]{1,0:T(8,128)(2,1)S(1)}, bf16[3456,256]{1,0:T(8,128)(2,1)S(1)}, bf16[512,2048]{1,0:T(8,128)(2,1)S(1)}, bf16[1024,256]{1,0:T(8,128)(2,...) custom-call(f32[12582912]{0:T(1024)} %begin.1.begun, bf16[8,16,2048]{2,1,0:T(8,128)(2,1)S(1)} %copy-done, ...), custom_call_target="tpu_custom_call" | custom-call | flops 100000000 | bytes 8388608 | tf_op jit(solution)/shard_map/before/pallas_call | solution.py:159
  9.5 0.1 pad_add_fusion.where
  9.5 0.0 collective-permute-done.xb
  9.5 0.0 collective-permute-done.1.xa
  9.5 0.8 %columns.1 = (bf16[32,2048]{1,0:T(8,128)(2,1)S(1)}, bf16[32,2048]{1,0:T(8,128)(2,1)S(1)}) custom-call(s32[4]{0:T(128)S(1)} %pad_add_fusion.where, bf16[8,16,2048]{2,1,0:T(8,128)(2,1)S(1)} %copy-done, bf16[2,16,2048]{2,1,0:T(8,128)(2,1)S(1)} %collective-permute-done.xb, bf16[2,16,2048]{2,1,0:T(8,128)(2,1)S(1)} %collective-permute-done.1.xa), custom_call_target="tpu_custom_call" | custom-call | tf_op jit(solution)/shard_map/columns/pallas_call | solution.py:213
  10.4 1.3 %collective-permute-start.2 = (bf16[32,2048]{1,0:T(8,128)(2,1)S(1)}, bf16[32,2048]{1,0:T(8,128)(2,1)S(1)}, u32[]{:S(2)}, u32[]{:S(2)}) collective-permute-start(bf16[32,2048]{1,0:T(8,128)(2,1)S(1)} %get-tuple-element.23.near), channel_id=1, source_target_pairs={{0,1},{1,0},{2,3},{3,2},{4,5},{5,4},{6,7},{7,6},{8,9},{9,8},{10,11... | collective-permute-start | bytes 393224 | tf_op jit(solution)/shard_map/ppermute | solution.py:421
  11.7 3.4 %collective-permute-start.3 = (bf16[32,2048]{1,0:T(8,128)(2,1)S(1)}, bf16[32,2048]{1,0:T(8,128)(2,1)S(1)}, u32[]{:S(2)}, u32[]{:S(2)}) collective-permute-start(bf16[32,2048]{1,0:T(8,128)(2,1)S(1)} %get-tuple-element.24.far), channel_id=1, source_target_pairs={{1,2},{2,1},{3,4},{4,3},{5,6},{6,5},{9,10},{10,9},{11,12},{12,11},... | collective-permute-start | bytes 393224 | tf_op jit(solution)/shard_map/ppermute | solution.py:420
  15.2 2.1 %slabs.1 = (bf16[160,2176]{1,0:T(8,128)(2,1)S(1)}, bf16[160,2176]{1,0:T(8,128)(2,1)S(1)}, bf16[160,2176]{1,0:T(8,128)(2,1)S(1)}, bf16[128,2048]{1,0:T(8,128)(2,1)S(1)}, bf16[3,64,2176]{2,1,0:T(8,128)(2,1)S(1)}) custom-call(s32[4]{0:T(128)S(1)} %pad_add_fusion.where, bf16[8,16,2048]{2,1,0:T(8,128)(2,1)S(1)} %copy-done, ...), custom_call_target="tpu_custom_call" | custom-call | flops 2000000000 | bytes 1048576 | tf_op jit(solution)/shard_map/slabs/pallas_call | solution.py:255
  17.3 0.0 collective-permute-done.2.ya
  17.3 0.7 %collective-permute-done.3.yb = bf16[32,2048]{1,0:T(8,128)(2,1)S(1)} collective-permute-done((bf16[32,2048]{1,0:T(8,128)(2,1)S(1)}, bf16[32,2048]{1,0:T(8,128)(2,1)S(1)}, u32[]{:S(2)}, u32[]{:S(2)}) %collective-permute-start.3) | collective-permute-done | bytes 131104 | tf_op jit(solution)/shard_map/ppermute | solution.py:420
  18.0 2.0 %outer.1 = (bf16[160,2176]{1,0:T(8,128)(2,1)S(1)}, bf16[160,2176]{1,0:T(8,128)(2,1)S(1)}, bf16[160,2176]{1,0:T(8,128)(2,1)S(1)}, bf16[128,2048]{1,0:T(8,128)(2,1)S(1)}) custom-call(s32[4]{0:T(128)S(1)} %pad_add_fusion.where, bf16[160,2176]{1,0:T(8,128)(2,1)S(1)} %get-tuple-element.26.a0i, ...), custom_call_target="tpu_custom_call", output_to_operand_aliasing={{0}: (1, {}), {1}: (2, {}), {2}: (3, {}), {3}: (4, {})} | custom-call | tf_op jit(solution)/shard_map/outer/pallas_call | solution.py:327
  20.0 0.0 copy-start.4
  20.0 0.0 copy-start.6
  20.0 3.3 %second.1 = bf16[1024,128]{1,0:T(8,128)(2,1)S(1)} custom-call(bf16[160,2176]{1,0:T(8,128)(2,1)S(1)} %get-tuple-element.31.a0, bf16[160,2176]{1,0:T(8,128)(2,1)S(1)} %get-tuple-element.32.a1, bf16[160,2176]{1,0:T(8,128)(2,1)S(1)} %get-tuple-element.33.a2, bf16[128,2048]{1,0:T(8,128)(2,1)S(1)} %get-tuple-element.34.own, ...), custom_call_target="tpu_custom_call" | custom-call | tf_op jit(solution)/shard_map/second/pallas_call | solution.py:337
  23.3 21.4 %all_to_all.5 = bf16[128,8,128]{2,1,0:T(8,128)(2,1)S(1)} all-to-all(bf16[128,8,128]{2,1,0:T(8,128)(2,1)S(1)} %bitcast.7), channel_id=1, replica_groups=mesh['gx'=16,'gy'=8] {'gx','gy'}, dimensions={0} | all-to-all | bytes 524288 | tf_op jit(solution)/shard_map/all_to_all | solution.py:425
  44.7 0.0 copy-done.4
  44.7 0.0 copy-done.6
  44.7 1.2 %head.1 = bf16[64,128]{1,0:T(8,128)(2,1)} custom-call(bf16[1024,128]{1,0:T(8,128)(2,1)S(1)} %bitcast.8, bf16[64,256]{1,0:T(8,128)(2,1)S(1)} %copy-done.6, bf16[256,128]{1,0:T(8,128)(2,1)S(1)} %copy-done.4), custom_call_target="tpu_custom_call" | custom-call | tf_op jit(solution)/shard_map/head/pallas_call | solution.py:388
  (1 shorter events, 0.0 us)
Async XLA Ops:
  1.0 8.5 %collective-permute-start = (bf16[2,16,2048]{2,1,0:T(8,128)(2,1)S(1)}, bf16[2,16,2048]{2,1,0:T(8,128)(2,1)S(1)}, u32[]{:S(2)}, u32[]{:S(2)}) collective-permute-start(bf16[2,16,2048]{2,1,0:T(8,128)(2,1)S(1)} %get-tuple-element.40), channel_id=1, source_target_pairs={{8,16},{16,8},{24,32},{32,24},{40,48},{48,40},{56,64},{64,56},{72,... | collective-permute-start | bytes 393224 | tf_op jit(solution)/shard_map/ppermute | solution.py:414
  1.7 4.6 %copy-start = (bf16[8,16,2048]{2,1,0:T(8,128)(2,1)S(1)}, bf16[8,16,2048]{2,1,0:T(8,128)(2,1)}, u32[]{:S(2)}) copy-start(bf16[8,16,2048]{2,1,0:T(8,128)(2,1)} %v.5) | copy-start | bytes 1572868
  1.7 4.6 %copy-start.1 = (bf16[1728,64]{0,1:T(8,128)(2,1)S(1)}, bf16[1728,64]{0,1:T(8,128)(2,1)}, u32[]{:S(2)}) copy-start(bf16[1728,64]{0,1:T(8,128)(2,1)} %param.12) | copy-start | bytes 663556
  1.7 4.6 %copy-start.2 = (bf16[1728,64]{0,1:T(8,128)(2,1)S(1)}, bf16[1728,64]{0,1:T(8,128)(2,1)}, u32[]{:S(2)}) copy-start(bf16[1728,64]{0,1:T(8,128)(2,1)} %param.13) | copy-start | bytes 663556
  1.7 4.6 %copy-start.3 = (s32[8,16,32]{2,1,0:T(8,128)S(1)}, s32[8,16,32]{2,1,0:T(8,128)}, u32[]{:S(2)}) copy-start(s32[8,16,32]{2,1,0:T(8,128)} %labels.1) | copy-start | bytes 49156
  1.7 4.6 %copy-start.5 = (s32[8192]{0:T(1024)S(1)}, s32[8192]{0:T(1024)}, u32[]{:S(2)}) copy-start(s32[8192]{0:T(1024)} %param.11) | copy-start | bytes 98308
  1.7 4.6 %copy-start.7 = (s32[1,256]{1,0:T(1,128)S(1)}, s32[1,256]{1,0:T(1,128)}, u32[]{:S(2)}) copy-start(s32[1,256]{1,0:T(1,128)} %lists.1) | copy-start | bytes 3076
  1.7 7.8 %collective-permute-start.1 = (bf16[2,16,2048]{2,1,0:T(8,128)(2,1)S(1)}, bf16[2,16,2048]{2,1,0:T(8,128)(2,1)S(1)}, u32[]{:S(2)}, u32[]{:S(2)}) collective-permute-start(bf16[2,16,2048]{2,1,0:T(8,128)(2,1)S(1)} %get-tuple-element.39), channel_id=1, source_target_pairs={{0,8},{8,0},{16,24},{24,16},{32,40},{40,32},{48,56},{56,48},{64,72... | collective-permute-start | bytes 393224 | tf_op jit(solution)/shard_map/ppermute | solution.py:415
  10.4 6.9 %collective-permute-start.2 = (bf16[32,2048]{1,0:T(8,128)(2,1)S(1)}, bf16[32,2048]{1,0:T(8,128)(2,1)S(1)}, u32[]{:S(2)}, u32[]{:S(2)}) collective-permute-start(bf16[32,2048]{1,0:T(8,128)(2,1)S(1)} %get-tuple-element.23.near), channel_id=1, source_target_pairs={{0,1},{1,0},{2,3},{3,2},{4,5},{5,4},{6,7},{7,6},{8,9},{9,8},{10,11... | collective-permute-start | bytes 393224 | tf_op jit(solution)/shard_map/ppermute | solution.py:421
  11.7 6.3 %collective-permute-start.3 = (bf16[32,2048]{1,0:T(8,128)(2,1)S(1)}, bf16[32,2048]{1,0:T(8,128)(2,1)S(1)}, u32[]{:S(2)}, u32[]{:S(2)}) collective-permute-start(bf16[32,2048]{1,0:T(8,128)(2,1)S(1)} %get-tuple-element.24.far), channel_id=1, source_target_pairs={{1,2},{2,1},{3,4},{4,3},{5,6},{6,5},{9,10},{10,9},{11,12},{12,11},... | collective-permute-start | bytes 393224 | tf_op jit(solution)/shard_map/ppermute | solution.py:420
  20.0 24.7 %copy-start.4 = (bf16[256,128]{1,0:T(8,128)(2,1)S(1)}, bf16[256,128]{1,0:T(8,128)(2,1)}, u32[]{:S(2)}) copy-start(bf16[256,128]{1,0:T(8,128)(2,1)} %w_out.1) | copy-start | bytes 196612
  20.0 24.7 %copy-start.6 = (bf16[64,256]{1,0:T(8,128)(2,1)S(1)}, bf16[64,256]{1,0:T(8,128)(2,1)}, u32[]{:S(2)}) copy-start(bf16[64,256]{1,0:T(8,128)(2,1)} %w_in.1) | copy-start | bytes 98308

commit v4 on v3

--- a/solution.py
+++ b/solution.py
@@ -53,6 +53,11 @@
         cost_estimate=pl.CostEstimate(flops=10**10, bytes_accessed=4096, transcendentals=0),
         name="begin",
     )()
+
+
+def column_of(r):
+    c, x = r // 16, r % 16
+    return c, x, jnp.where(c < 2, c, c + SY - 4)
 
 
 def band(wt_ref, out_ref):
@@ -91,11 +96,11 @@
     return below, wide, above
 
 
-def windows(shifted, starts, rows):
+def convolve(shifted, starts, rows, weight, step):
     parts = []
-    for b in range(NB):
-        for start in starts:
-            parts.append(
+    for first in range(0, NB, step):
+        left = jnp.concatenate(
+            [
                 jnp.concatenate(
                     [
                         ref[start + kx * SY : start + kx * SY + rows, 256 * b : 256 * b + 384]
@@ -104,18 +109,26 @@
                     ],
                     axis=1,
                 )
-            )
+                for b in range(first, first + step)
+                for start in starts
+            ],
+            axis=0,
+        )
+        parts.append(dot(left, weight[...]))
     return jnp.concatenate(parts, axis=0)
 
 
-def before_kernel(begun, v, labels, lists, home, w1t, w2t, wb1, wb2, member, place, meta, core, s0, s1, s2):
+def before_kernel(begun, v, labels, lists, home, w1t, w2t, wb1, wb2, member, place, meta, core, mine, s0, s1, s2):
     slots = lists.shape[1]
     band(w1t, wb1)
     own = v[...].reshape(SX * SY, LANES)
     s0[...], s1[...], s2[...] = shifts_y(widen(relu(own)))
-    conv = dot(windows((s0, s1, s2), (0,), (SX - 2) * SY), wb1[...])
+    conv = convolve((s0, s1, s2), (0,), (SX - 2) * SY, wb1, 4)
     core[...] = (conv + blocks(own[SY : SX * SY - SY]).astype(F32)).astype(BF16)
     band(w2t, wb2)
+    c, x, y = column_of(iota((64, SX * SY), 0))
+    pick = ((x - 2) * SY + y == iota((64, SX * SY), 1)) & (x >= 2) & (x < EX - 2)
+    mine[...] = dot(pick.astype(F32).astype(BF16), own)
     lab = labels[...].reshape(SX * SY, SZ).T
     ids = iota((slots, SX * SY), 0)
     count = jnp.zeros((slots, SX * SY), F32)
@@ -165,9 +178,10 @@
             jax.ShapeDtypeStruct((devices * CAP, slots), BF16),
             jax.ShapeDtypeStruct((slots, 128), BF16),
             jax.ShapeDtypeStruct((NB * (SX - 2) * SY, 256), BF16),
+            jax.ShapeDtypeStruct((64, LANES), F32),
         ),
         in_specs=[pl.BlockSpec(memory_space=pl.ANY)] + [VMEM] * 6,
-        out_specs=(VMEM,) * 6,
+        out_specs=(VMEM,) * 7,
         scratch_shapes=[pltpu.VMEM((SX * SY, WIDE), BF16)] * 3,
         compiler_params=params(),
         cost_estimate=pl.CostEstimate(flops=10**8, bytes_accessed=8 * 2**20, transcendentals=0),
@@ -179,23 +193,15 @@
     return jnp.where(flag, yes.astype(F32), no.astype(F32)).astype(BF16)
 
 
-def x_extended(even, v, xa, xb):
-    a = xa[...]
-    b = xb[...]
-    low = choose(even, b, a)
-    high = choose(even, a, b)
-    return jnp.concatenate([low, v[...], high], axis=0)
-
-
-def columns_kernel(where, v, xb, xa, near, far):
+def columns_kernel(where, mine, xb, xa, near, far):
     x_even = where[0] % 2 == 0
     y_even = where[1] % 2 == 0
-    block = x_extended(x_even, v, xa, xb).reshape(EX * SY, LANES)
-    r = iota((64, EX * SY), 0)
-    c = r // 16
-    y = jnp.where(c < 2, c, c + 12)
-    pick = ((r % 16) * 16 + y == iota((64, EX * SY), 1)).astype(F32).astype(BF16)
-    cols = dot(pick, block).astype(BF16)
+    sides = jnp.concatenate([xa[...], xb[...]], axis=0).reshape(4 * SY, LANES)
+    c, x, y = column_of(iota((64, 4 * SY), 0))
+    k = jnp.where(x < 2, x, jnp.where((x >= EX - 2) & (x < EX), x - SX, -1))
+    k = jnp.where(x_even, jnp.where(k >= 2, k - 2, jnp.where(k >= 0, k + 2, -1)), k)
+    pick = ((k * SY + y == iota((64, 4 * SY), 1)) & (k >= 0)).astype(F32).astype(BF16)
+    cols = (mine[...] + dot(pick, sides)).astype(BF16)
 
     @pl.when(y_even)
     def _():
@@ -208,7 +214,7 @@
         far[...] = cols[32:64]
 
 
-def columns(where, v, xa, xb):
+def columns(where, mine, xb, xa):
     shape = jax.ShapeDtypeStruct((32, LANES), BF16)
     return pl.pallas_call(
         columns_kernel,
@@ -217,10 +223,10 @@
         out_specs=(VMEM, VMEM),
         compiler_params=params(),
         name="columns",
-    )(where, v, xb, xa)
-
-
-def slabs_kernel(where, v, xb, xa, core, near, far, wb, a0, a1, a2, own, cols, s0, s1, s2):
+    )(where, mine, xb, xa)
+
+
+def slabs_kernel(where, v, xa, xb, core, near, far, wb, a0, a1, a2, own, cols, raw, s0, s1, s2):
     gx, last_x = where[0], where[2] - 1
     x_even, y_even = where[0] % 2 == 0, where[1] % 2 == 0
     a, b = xa[...], xb[...]
@@ -228,7 +234,7 @@
         [choose(x_even, b, a), v[0:2], v[SX - 2 : SX], choose(x_even, a, b)], axis=0
     ).reshape(8 * SY, LANES)
     s0[...], s1[...], s2[...] = shifts_y(widen(relu(block)))
-    conv = dot(windows((s0, s1, s2), (0, 4 * SY), 2 * SY), wb[...])
+    conv = convolve((s0, s1, s2), (0, 4 * SY), 2 * SY, wb, 2)
     residual = jnp.concatenate([block[SY : 3 * SY], block[5 * SY : 7 * SY]], axis=0)
     x = iota((NB * 4 * SY, 256), 0) // SY % 4
     inside = ((x > 0) | (gx > 0)) & ((x < 3) | (gx < last_x))
@@ -239,7 +245,9 @@
     a0[...], a1[...], a2[...] = shifts_y(widen(relu(main)))
     low = choose(y_even, far[...], near[...])
     high = choose(y_even, near[...], far[...])
-    side = relu(jnp.concatenate([low, high], axis=0))
+    side = jnp.concatenate([low, high], axis=0)
+    raw[...] = side
+    side = relu(side)
     store_rolled(cols, widen(side))
 
 
@@ -260,26 +268,25 @@
             full,
             jax.ShapeDtypeStruct((SX * SY, LANES), BF16),
             jax.ShapeDtypeStruct((3, 64, WIDE), BF16),
+            jax.ShapeDtypeStruct((64, LANES), BF16),
         ),
         in_specs=[SMEM] + [VMEM] * 7,
-        out_specs=(VMEM,) * 5,
+        out_specs=(VMEM,) * 6,
         scratch_shapes=[pltpu.VMEM((8 * SY, WIDE), BF16)] * 3,
         compiler_params=params(),
         cost_estimate=pl.CostEstimate(flops=2 * 10**9, bytes_accessed=2**20, transcendentals=0),
         name="slabs",
-    )(where, v, xb, xa, core, near, far, wb)
+    )(where, v, xa, xb, core, near, far, wb)
 
 
 def outer_kernel(
-    where, a0i, a1i, a2i, owni, cols, near, far, ya, yb, wb1, a0, a1, a2, own, halo
+    where, a0i, a1i, a2i, owni, cols, raw, ya, yb, wb1, a0, a1, a2, own, halo
 ):
     gx, gy = where[0], where[1]
     last_x, last_y = where[2] - 1, where[3] - 1
     y_even = gy % 2 == 0
     low = choose(y_even, yb[...], ya[...])
     high = choose(y_even, ya[...], yb[...])
-    own_low = choose(y_even, far[...], near[...])
-    own_high = choose(y_even, near[...], far[...])
     store_rolled(halo, widen(relu(jnp.concatenate([low, high], axis=0))))
     at = [(halo, 0), (halo, 16), (cols, 0), (cols, 16), (cols, 32), (cols, 48), (halo, 32), (halo, 48)]
 
@@ -298,7 +305,7 @@
         axis=0,
     )
     conv = dot(left, wb1[...])
-    residual = jnp.concatenate([low[16:32], own_low[0:16], own_high[16:32], high[0:16]], axis=0)
+    residual = jnp.concatenate([low[16:32], raw[0:16], raw[48:64], high[0:16]], axis=0)
     residual = pltpu.roll(residual, 63, 0)
     row = iota((NB * 64, 256), 0)
     x = row % 16
@@ -322,18 +329,18 @@
         own[s + SY - 1 : s + SY] = edge[33 + x : 34 + x]
 
 
-def outer(where, a0, a1, a2, own, cols, near, far, ya, yb, wb1, wb2, member, place, meta):
+def outer(where, a0, a1, a2, own, cols, raw, ya, yb, wb1, wb2, member, place, meta):
     full = jax.ShapeDtypeStruct(a0.shape, BF16)
     a0, a1, a2, own = pl.pallas_call(
         outer_kernel,
         out_shape=(full, full, full, jax.ShapeDtypeStruct(own.shape, BF16)),
-        in_specs=[SMEM] + [VMEM] * 10,
+        in_specs=[SMEM] + [VMEM] * 9,
         out_specs=(VMEM,) * 4,
         scratch_shapes=[pltpu.VMEM((3, 64, WIDE), BF16)],
         input_output_aliases={1: 0, 2: 1, 3: 2, 4: 3},
         compiler_params=params(),
         name="outer",
-    )(where, a0, a1, a2, own, cols, near, far, ya, yb, wb1)
+    )(where, a0, a1, a2, own, cols, raw, ya, yb, wb1)
     return pl.pallas_call(
         second_kernel,
         out_shape=jax.ShapeDtypeStruct((place.shape[0], 128), BF16),
@@ -413,14 +420,14 @@
     inner_y, outer_y = pairs(n_gy)
     xb = lax.ppermute(to_b, "gx", outer_x)
     xa = lax.ppermute(to_a, "gx", inner_x)
-    wb1, wb2, member, place, meta, core = before(
+    wb1, wb2, member, place, meta, core, mine = before(
         begin(), features, labels, lists, home.reshape(-1, 128), conv_first.T, conv_second.T, devices
     )
-    near, far = columns(where, features, xa, xb)
+    near, far = columns(where, mine, xb, xa)
     yb = lax.ppermute(far, "gy", outer_y)
     ya = lax.ppermute(near, "gy", inner_y)
-    a0, a1, a2, own, cols = slabs(where, features, xa, xb, core, near, far, wb1)
-    rows = outer(where, a0, a1, a2, own, cols, near, far, ya, yb, wb1, wb2, member, place, meta)
+    a0, a1, a2, own, cols, raw = slabs(where, features, xa, xb, core, near, far, wb1)
+    rows = outer(where, a0, a1, a2, own, cols, raw, ya, yb, wb1, wb2, member, place, meta)
     rows = rows.reshape(devices, CAP, 128)
     got = lax.all_to_all(rows, ("gx", "gy"), 0, 0, tiled=True)
     return head(got.reshape(devices * CAP, 128), head_in, head_out, home.size // devices)

time: 46.2 us -> 46.1 us (level)
  no operation moved by 1% of the time
where the time goes in v4:
time: 46.1 us; the launch traced here: 45.9 us
  blocking collectives  21.4 us (46%)
  Pallas kernels  12.5 us (27%)
  starting transfers between devices  10 us (22%)
  local copies, waits for them, and re-layouts  1.04 us (2%)
  waiting for transfers between devices  0.81 us (2%)
    all_to_all x1, blocking collectives, local(): got = lax.all_to_all(rows, ('gx', 'gy'), 0, 0, tiled=True)  21.4 us
    ppermute x1, starting transfers between devices, local(): xa = lax.ppermute(to_a, 'gx', inner_x)  4.57 us
    ppermute x1, starting transfers between devices, local(): yb = lax.ppermute(far, 'gy', outer_y)  3.43 us
    pallas_call x1, Pallas kernels, outer(): pl.pallas_call(second_kernel, out_shape=jax.ShapeDtypeStruct((place.shape...  3.26 us
    pallas_call x1, Pallas kernels, before(): pl.pallas_call(before_kernel, out_shape=(jax.ShapeDtypeStruct((3456, 256)...  3.16 us
    pallas_call x1, Pallas kernels, outer(): pl.pallas_call(outer_kernel, out_shape=(full, full, full, jax.ShapeDtypeS...  2.03 us
    pallas_call x1, Pallas kernels, slabs(): pl.pallas_call(slabs_kernel, out_shape=(full, full, full, jax.ShapeDtypeS...  2.01 us
    ppermute x1, starting transfers between devices, local(): ya = lax.ppermute(near, 'gy', inner_y)  1.33 us
  transfers between devices with their start and end apart: 4, of which 1 were waited for; matrix products, arithmetic and copies ran while one was open for 0% of the time, Pallas kernels for 11%

profile of v4, /device:TPU:1, one launch (start us, length us, event | category | flops | bytes accessed | tf_op | source)
XLA Modules:
  0.0 45.9 jit_solution(145770087026303169)
XLA Ops:
  0.0 1.0 %constant_dynamic-slice_fusion = (bf16[2,16,2048]{2,1,0:T(8,128)(2,1)S(1)}, bf16[2,16,2048]{2,1,0:T(8,128)(2,1)S(1)}) fusion(bf16[8,16,2048]{2,1,0:T(8,128)(2,1)} %v.3, s32[]{:T(128)S(6)} %select_n.18, s32[]{:T(128)S(6)} %select_n.17), kind=kLoop, calls=%fused_computation.1 | loop fusion | bytes 524296 | tf_op jit(solution)/shard_map/dynamic_slice | solution.py:418
  1.0 0.7 %collective-permute-start.1 = (bf16[2,16,2048]{2,1,0:T(8,128)(2,1)S(1)}, bf16[2,16,2048]{2,1,0:T(8,128)(2,1)S(1)}, u32[]{:S(2)}, u32[]{:S(2)}) collective-permute-start(bf16[2,16,2048]{2,1,0:T(8,128)(2,1)S(1)} %get-tuple-element.43), channel_id=1, source_target_pairs={{8,16},{16,8},{24,32},{32,24},{40,48},{48,40},{56,64},{64,56},{72,... | collective-permute-start | bytes 393224 | tf_op jit(solution)/shard_map/ppermute | solution.py:421
  1.7 0.0 copy-start
  1.7 0.0 copy-start.1
  1.7 0.0 copy-start.2
  1.7 0.0 copy-start.3
  1.7 0.0 copy-start.5
  1.7 0.0 copy-start.7
  1.7 4.6 %collective-permute-start = (bf16[2,16,2048]{2,1,0:T(8,128)(2,1)S(1)}, bf16[2,16,2048]{2,1,0:T(8,128)(2,1)S(1)}, u32[]{:S(2)}, u32[]{:S(2)}) collective-permute-start(bf16[2,16,2048]{2,1,0:T(8,128)(2,1)S(1)} %get-tuple-element.44), channel_id=1, source_target_pairs={{0,8},{8,0},{16,24},{24,16},{32,40},{40,32},{48,56},{56,48},{64,72... | collective-permute-start | bytes 393224 | tf_op jit(solution)/shard_map/ppermute | solution.py:422
  6.3 0.0 copy-done
  6.3 0.0 copy-done.1
  6.3 0.0 copy-done.2
  6.3 0.0 copy-done.3
  6.3 0.0 copy-done.5
  6.3 0.0 copy-done.7
  6.4 3.2 %before.1 = (bf16[3456,256]{1,0:T(8,128)(2,1)S(1)}, bf16[3456,256]{1,0:T(8,128)(2,1)S(1)}, bf16[512,2048]{1,0:T(8,128)(2,1)S(1)}, bf16[1024,256]{1,0:T(8,128)(2,...) custom-call(f32[12582912]{0:T(1024)} %begin.1.begun, ...), custom_call_target="tpu_custom_call" | custom-call | flops 100000000 | bytes 8388608 | tf_op jit(solution)/shard_map/before/pallas_call | solution.py:172
  9.5 0.1 pad_add_fusion.where
  9.6 0.0 collective-permute-done.1.xb
  9.6 0.0 collective-permute-done.xa
  9.6 0.8 %columns.1 = (bf16[32,2048]{1,0:T(8,128)(2,1)S(1)}, bf16[32,2048]{1,0:T(8,128)(2,1)S(1)}) custom-call(s32[4]{0:T(128)S(1)} %pad_add_fusion.where, f32[64,2048]{1,0:T(8,128)S(1)} %get-tuple-element.25.mine, bf16[2,16,2048]{2,1,0:T(8,128)(2,1)S(1)} %collective-permute-done.1.xb, bf16[2,16,2048]{2,1,0:T(8,128)(2,1)S(1)} %collective-permute-done.xa), custom_call_target="tpu_custom_call" | custom-call | tf_op jit(solution)/shard_map/columns/pallas_call | solution.py:219
  10.4 1.3 %collective-permute-start.2 = (bf16[32,2048]{1,0:T(8,128)(2,1)S(1)}, bf16[32,2048]{1,0:T(8,128)(2,1)S(1)}, u32[]{:S(2)}, u32[]{:S(2)}) collective-permute-start(bf16[32,2048]{1,0:T(8,128)(2,1)S(1)} %get-tuple-element.26.near), channel_id=1, source_target_pairs={{0,1},{1,0},{2,3},{3,2},{4,5},{5,4},{6,7},{7,6},{8,9},{9,8},{10,11... | collective-permute-start | bytes 393224 | tf_op jit(solution)/shard_map/ppermute | solution.py:428
  11.7 3.4 %collective-permute-start.3 = (bf16[32,2048]{1,0:T(8,128)(2,1)S(1)}, bf16[32,2048]{1,0:T(8,128)(2,1)S(1)}, u32[]{:S(2)}, u32[]{:S(2)}) collective-permute-start(bf16[32,2048]{1,0:T(8,128)(2,1)S(1)} %get-tuple-element.27.far), channel_id=1, source_target_pairs={{1,2},{2,1},{3,4},{4,3},{5,6},{6,5},{9,10},{10,9},{11,12},{12,11},... | collective-permute-start | bytes 393224 | tf_op jit(solution)/shard_map/ppermute | solution.py:427
  15.2 2.0 %slabs.1 = (bf16[160,2176]{1,0:T(8,128)(2,1)S(1)}, bf16[160,2176]{1,0:T(8,128)(2,1)S(1)}, bf16[160,2176]{1,0:T(8,128)(2,1)S(1)}, bf16[128,2048]{1,0:T(8,128)(2,1...) custom-call(s32[4]{0:T(128)S(1)} %pad_add_fusion.where, bf16[8,16,2048]{2,1,0:T(8,128)(2,1)S(1)} %copy-done, ...), custom_call_target="tpu_custom_call" | custom-call | flops 2000000000 | bytes 1048576 | tf_op jit(solution)/shard_map/slabs/pallas_call | solution.py:263
  17.2 0.0 collective-permute-done.2.ya
  17.2 0.8 %collective-permute-done.3.yb = bf16[32,2048]{1,0:T(8,128)(2,1)S(1)} collective-permute-done((bf16[32,2048]{1,0:T(8,128)(2,1)S(1)}, bf16[32,2048]{1,0:T(8,128)(2,1)S(1)}, u32[]{:S(2)}, u32[]{:S(2)}) %collective-permute-start.3) | collective-permute-done | bytes 131104 | tf_op jit(solution)/shard_map/ppermute | solution.py:427
  18.0 2.0 %outer.1 = (bf16[160,2176]{1,0:T(8,128)(2,1)S(1)}, bf16[160,2176]{1,0:T(8,128)(2,1)S(1)}, bf16[160,2176]{1,0:T(8,128)(2,1)S(1)}, bf16[128,2048]{1,0:T(8,128)(2,1)S(1)}) custom-call(s32[4]{0:T(128)S(1)} %pad_add_fusion.where, bf16[160,2176]{1,0:T(8,128)(2,1)S(1)} %get-tuple-element.29.a0i, ...), custom_call_target="tpu_custom_call", output_to_operand_aliasing={{0}: (1, {}), {1}: (2, {}), {2}: (3, {}), {3}: (4, {})} | custom-call | tf_op jit(solution)/shard_map/outer/pallas_call | solution.py:334
  20.0 0.0 copy-start.4
  20.0 0.0 copy-start.6
  20.1 3.3 %second.1 = bf16[1024,128]{1,0:T(8,128)(2,1)S(1)} custom-call(bf16[160,2176]{1,0:T(8,128)(2,1)S(1)} %get-tuple-element.35.a0, bf16[160,2176]{1,0:T(8,128)(2,1)S(1)} %get-tuple-element.36.a1, bf16[160,2176]{1,0:T(8,128)(2,1)S(1)} %get-tuple-element.37.a2, bf16[128,2048]{1,0:T(8,128)(2,1)S(1)} %get-tuple-element.38.own, ...), custom_call_target="tpu_custom_call" | custom-call | tf_op jit(solution)/shard_map/second/pallas_call | solution.py:344
  23.3 21.4 %all_to_all.5 = bf16[128,8,128]{2,1,0:T(8,128)(2,1)S(1)} all-to-all(bf16[128,8,128]{2,1,0:T(8,128)(2,1)S(1)} %bitcast.7), channel_id=1, replica_groups=mesh['gx'=16,'gy'=8] {'gx','gy'}, dimensions={0} | all-to-all | bytes 524288 | tf_op jit(solution)/shard_map/all_to_all | solution.py:432
  44.7 0.0 copy-done.4
  44.7 0.0 copy-done.6
  44.7 1.2 %head.1 = bf16[64,128]{1,0:T(8,128)(2,1)} custom-call(bf16[1024,128]{1,0:T(8,128)(2,1)S(1)} %bitcast.8, bf16[64,256]{1,0:T(8,128)(2,1)S(1)} %copy-done.6, bf16[256,128]{1,0:T(8,128)(2,1)S(1)} %copy-done.4), custom_call_target="tpu_custom_call" | custom-call | tf_op jit(solution)/shard_map/head/pallas_call | solution.py:395
  (1 shorter events, 0.0 us)
Async XLA Ops:
  1.0 8.6 %collective-permute-start.1 = (bf16[2,16,2048]{2,1,0:T(8,128)(2,1)S(1)}, bf16[2,16,2048]{2,1,0:T(8,128)(2,1)S(1)}, u32[]{:S(2)}, u32[]{:S(2)}) collective-permute-start(bf16[2,16,2048]{2,1,0:T(8,128)(2,1)S(1)} %get-tuple-element.43), channel_id=1, source_target_pairs={{8,16},{16,8},{24,32},{32,24},{40,48},{48,40},{56,64},{64,56},{72,... | collective-permute-start | bytes 393224 | tf_op jit(solution)/shard_map/ppermute | solution.py:421
  1.7 4.6 %copy-start = (bf16[8,16,2048]{2,1,0:T(8,128)(2,1)S(1)}, bf16[8,16,2048]{2,1,0:T(8,128)(2,1)}, u32[]{:S(2)}) copy-start(bf16[8,16,2048]{2,1,0:T(8,128)(2,1)} %v.3) | copy-start | bytes 1572868
  1.7 4.6 %copy-start.1 = (bf16[1728,64]{0,1:T(8,128)(2,1)S(1)}, bf16[1728,64]{0,1:T(8,128)(2,1)}, u32[]{:S(2)}) copy-start(bf16[1728,64]{0,1:T(8,128)(2,1)} %param.12) | copy-start | bytes 663556
  1.7 4.6 %copy-start.2 = (bf16[1728,64]{0,1:T(8,128)(2,1)S(1)}, bf16[1728,64]{0,1:T(8,128)(2,1)}, u32[]{:S(2)}) copy-start(bf16[1728,64]{0,1:T(8,128)(2,1)} %param.13) | copy-start | bytes 663556
  1.7 4.6 %copy-start.3 = (s32[8,16,32]{2,1,0:T(8,128)S(1)}, s32[8,16,32]{2,1,0:T(8,128)}, u32[]{:S(2)}) copy-start(s32[8,16,32]{2,1,0:T(8,128)} %labels.1) | copy-start | bytes 49156
  1.7 4.6 %copy-start.5 = (s32[8192]{0:T(1024)S(1)}, s32[8192]{0:T(1024)}, u32[]{:S(2)}) copy-start(s32[8192]{0:T(1024)} %param.11) | copy-start | bytes 98308
  1.7 4.6 %copy-start.7 = (s32[1,256]{1,0:T(1,128)S(1)}, s32[1,256]{1,0:T(1,128)}, u32[]{:S(2)}) copy-start(s32[1,256]{1,0:T(1,128)} %lists.1) | copy-start | bytes 3076
  1.7 7.9 %collective-permute-start = (bf16[2,16,2048]{2,1,0:T(8,128)(2,1)S(1)}, bf16[2,16,2048]{2,1,0:T(8,128)(2,1)S(1)}, u32[]{:S(2)}, u32[]{:S(2)}) collective-permute-start(bf16[2,16,2048]{2,1,0:T(8,128)(2,1)S(1)} %get-tuple-element.44), channel_id=1, source_target_pairs={{0,8},{8,0},{16,24},{24,16},{32,40},{40,32},{48,56},{56,48},{64,72... | collective-permute-start | bytes 393224 | tf_op jit(solution)/shard_map/ppermute | solution.py:422
  10.4 6.8 %collective-permute-start.2 = (bf16[32,2048]{1,0:T(8,128)(2,1)S(1)}, bf16[32,2048]{1,0:T(8,128)(2,1)S(1)}, u32[]{:S(2)}, u32[]{:S(2)}) collective-permute-start(bf16[32,2048]{1,0:T(8,128)(2,1)S(1)} %get-tuple-element.26.near), channel_id=1, source_target_pairs={{0,1},{1,0},{2,3},{3,2},{4,5},{5,4},{6,7},{7,6},{8,9},{9,8},{10,11... | collective-permute-start | bytes 393224 | tf_op jit(solution)/shard_map/ppermute | solution.py:428
  11.7 6.3 %collective-permute-start.3 = (bf16[32,2048]{1,0:T(8,128)(2,1)S(1)}, bf16[32,2048]{1,0:T(8,128)(2,1)S(1)}, u32[]{:S(2)}, u32[]{:S(2)}) collective-permute-start(bf16[32,2048]{1,0:T(8,128)(2,1)S(1)} %get-tuple-element.27.far), channel_id=1, source_target_pairs={{1,2},{2,1},{3,4},{4,3},{5,6},{6,5},{9,10},{10,9},{11,12},{12,11},... | collective-permute-start | bytes 393224 | tf_op jit(solution)/shard_map/ppermute | solution.py:427
  20.0 24.7 %copy-start.4 = (bf16[256,128]{1,0:T(8,128)(2,1)S(1)}, bf16[256,128]{1,0:T(8,128)(2,1)}, u32[]{:S(2)}) copy-start(bf16[256,128]{1,0:T(8,128)(2,1)} %w_out.1) | copy-start | bytes 196612
  20.0 24.6 %copy-start.6 = (bf16[64,256]{1,0:T(8,128)(2,1)S(1)}, bf16[64,256]{1,0:T(8,128)(2,1)}, u32[]{:S(2)}) copy-start(bf16[64,256]{1,0:T(8,128)(2,1)} %w_in.1) | copy-start | bytes 98308

commit v5 on v4

--- a/solution.py
+++ b/solution.py
@@ -56,7 +56,7 @@
 
 
 def column_of(r):
-    c, x = r // 16, r % 16
+    c, x = r // EX, r % EX
     return c, x, jnp.where(c < 2, c, c + SY - 4)
 
 
@@ -126,8 +126,8 @@
     conv = convolve((s0, s1, s2), (0,), (SX - 2) * SY, wb1, 4)
     core[...] = (conv + blocks(own[SY : SX * SY - SY]).astype(F32)).astype(BF16)
     band(w2t, wb2)
-    c, x, y = column_of(iota((64, SX * SY), 0))
-    pick = ((x - 2) * SY + y == iota((64, SX * SY), 1)) & (x >= 2) & (x < EX - 2)
+    c, x, y = column_of(iota((4 * EX, SX * SY), 0))
+    pick = ((x - 2) * SY + y == iota((4 * EX, SX * SY), 1)) & (x >= 2) & (x < EX - 2)
     mine[...] = dot(pick.astype(F32).astype(BF16), own)
     lab = labels[...].reshape(SX * SY, SZ).T
     ids = iota((slots, SX * SY), 0)
@@ -178,7 +178,7 @@
             jax.ShapeDtypeStruct((devices * CAP, slots), BF16),
             jax.ShapeDtypeStruct((slots, 128), BF16),
             jax.ShapeDtypeStruct((NB * (SX - 2) * SY, 256), BF16),
-            jax.ShapeDtypeStruct((64, LANES), F32),
+            jax.ShapeDtypeStruct((4 * EX, LANES), F32),
         ),
         in_specs=[pl.BlockSpec(memory_space=pl.ANY)] + [VMEM] * 6,
         out_specs=(VMEM,) * 7,
@@ -193,29 +193,35 @@
     return jnp.where(flag, yes.astype(F32), no.astype(F32)).astype(BF16)
 
 
+def choose_columns(flag, yes, no):
+    both = jnp.where(flag, yes.astype(F32), no.astype(F32))
+    zero = jnp.zeros((16 - EX, LANES), F32)
+    return jnp.concatenate([both[:EX], zero, both[EX:], zero], axis=0).astype(BF16)
+
+
 def columns_kernel(where, mine, xb, xa, near, far):
     x_even = where[0] % 2 == 0
     y_even = where[1] % 2 == 0
     sides = jnp.concatenate([xa[...], xb[...]], axis=0).reshape(4 * SY, LANES)
-    c, x, y = column_of(iota((64, 4 * SY), 0))
+    c, x, y = column_of(iota((4 * EX, 4 * SY), 0))
     k = jnp.where(x < 2, x, jnp.where((x >= EX - 2) & (x < EX), x - SX, -1))
     k = jnp.where(x_even, jnp.where(k >= 2, k - 2, jnp.where(k >= 0, k + 2, -1)), k)
-    pick = ((k * SY + y == iota((64, 4 * SY), 1)) & (k >= 0)).astype(F32).astype(BF16)
+    pick = ((k * SY + y == iota((4 * EX, 4 * SY), 1)) & (k >= 0)).astype(F32).astype(BF16)
     cols = (mine[...] + dot(pick, sides)).astype(BF16)
 
     @pl.when(y_even)
     def _():
-        near[...] = cols[32:64]
-        far[...] = cols[0:32]
+        near[...] = cols[2 * EX :]
+        far[...] = cols[: 2 * EX]
 
     @pl.when(jnp.logical_not(y_even))
     def _():
-        near[...] = cols[0:32]
-        far[...] = cols[32:64]
+        near[...] = cols[: 2 * EX]
+        far[...] = cols[2 * EX :]
 
 
 def columns(where, mine, xb, xa):
-    shape = jax.ShapeDtypeStruct((32, LANES), BF16)
+    shape = jax.ShapeDtypeStruct((2 * EX, LANES), BF16)
     return pl.pallas_call(
         columns_kernel,
         out_shape=(shape, shape),
@@ -243,8 +249,8 @@
     main = jnp.concatenate([sides[0 : 2 * SY], unblocks(core[...]), sides[2 * SY :]], axis=0)
     own[...] = main[SY : SY + SX * SY]
     a0[...], a1[...], a2[...] = shifts_y(widen(relu(main)))
-    low = choose(y_even, far[...], near[...])
-    high = choose(y_even, near[...], far[...])
+    low = choose_columns(y_even, far[...], near[...])
+    high = choose_columns(y_even, near[...], far[...])
     side = jnp.concatenate([low, high], axis=0)
     raw[...] = side
     side = relu(side)
@@ -285,8 +291,8 @@
     gx, gy = where[0], where[1]
     last_x, last_y = where[2] - 1, where[3] - 1
     y_even = gy % 2 == 0
-    low = choose(y_even, yb[...], ya[...])
-    high = choose(y_even, ya[...], yb[...])
+    low = choose_columns(y_even, yb[...], ya[...])
+    high = choose_columns(y_even, ya[...], yb[...])
     store_rolled(halo, widen(relu(jnp.concatenate([low, high], axis=0))))
     at = [(halo, 0), (halo, 16), (cols, 0), (cols, 16), (cols, 32), (cols, 48), (halo, 32), (halo, 48)]
 

time: 46.1 us -> 45.7 us (level)
  no operation moved by 1% of the time
where the time goes in v5:
time: 45.7 us; the launch traced here: 45.6 us
  blocking collectives  21.4 us (47%)
  Pallas kernels  12.5 us (27%)
  starting transfers between devices  10 us (22%)
  local copies, waits for them, and re-layouts  1.04 us (2%)
  waiting for transfers between devices  0.46 us (1%)
    all_to_all x1, blocking collectives, local(): got = lax.all_to_all(rows, ('gx', 'gy'), 0, 0, tiled=True)  21.4 us
    ppermute x1, starting transfers between devices, local(): xa = lax.ppermute(to_a, 'gx', inner_x)  4.57 us
    ppermute x1, starting transfers between devices, local(): yb = lax.ppermute(far, 'gy', outer_y)  3.43 us
    pallas_call x1, Pallas kernels, outer(): pl.pallas_call(second_kernel, out_shape=jax.ShapeDtypeStruct((place.shape...  3.25 us
    pallas_call x1, Pallas kernels, before(): pl.pallas_call(before_kernel, out_shape=(jax.ShapeDtypeStruct((3456, 256)...  3.16 us
    pallas_call x1, Pallas kernels, outer(): pl.pallas_call(outer_kernel, out_shape=(full, full, full, jax.ShapeDtypeS...  2.03 us
    pallas_call x1, Pallas kernels, slabs(): pl.pallas_call(slabs_kernel, out_shape=(full, full, full, jax.ShapeDtypeS...  2.01 us
    ppermute x1, starting transfers between devices, local(): ya = lax.ppermute(near, 'gy', inner_y)  1.33 us
  transfers between devices with their start and end apart: 4, of which 1 were waited for; matrix products, arithmetic and copies ran while one was open for 0% of the time, Pallas kernels for 11%

profile of v5, /device:TPU:1, one launch (start us, length us, event | category | flops | bytes accessed | tf_op | source)
XLA Modules:
  0.0 45.6 jit_solution(7757263276608780471)
XLA Ops:
  0.0 1.0 %constant_dynamic-slice_fusion = (bf16[2,16,2048]{2,1,0:T(8,128)(2,1)S(1)}, bf16[2,16,2048]{2,1,0:T(8,128)(2,1)S(1)}) fusion(bf16[8,16,2048]{2,1,0:T(8,128)(2,1)} %v.3, s32[]{:T(128)S(6)} %select_n.18, s32[]{:T(128)S(6)} %select_n.17), kind=kLoop, calls=%fused_computation.1 | loop fusion | bytes 524296 | tf_op jit(solution)/shard_map/dynamic_slice | solution.py:424
  1.0 0.7 %collective-permute-start.1 = (bf16[2,16,2048]{2,1,0:T(8,128)(2,1)S(1)}, bf16[2,16,2048]{2,1,0:T(8,128)(2,1)S(1)}, u32[]{:S(2)}, u32[]{:S(2)}) collective-permute-start(bf16[2,16,2048]{2,1,0:T(8,128)(2,1)S(1)} %get-tuple-element.43), channel_id=1, source_target_pairs={{8,16},{16,8},{24,32},{32,24},{40,48},{48,40},{56,64},{64,56},{72,... | collective-permute-start | bytes 393224 | tf_op jit(solution)/shard_map/ppermute | solution.py:427
  1.7 0.0 copy-start
  1.7 0.0 copy-start.1
  1.7 0.0 copy-start.2
  1.7 0.0 copy-start.3
  1.7 0.0 copy-start.5
  1.7 0.0 copy-start.7
  1.7 4.6 %collective-permute-start = (bf16[2,16,2048]{2,1,0:T(8,128)(2,1)S(1)}, bf16[2,16,2048]{2,1,0:T(8,128)(2,1)S(1)}, u32[]{:S(2)}, u32[]{:S(2)}) collective-permute-start(bf16[2,16,2048]{2,1,0:T(8,128)(2,1)S(1)} %get-tuple-element.44), channel_id=1, source_target_pairs={{0,8},{8,0},{16,24},{24,16},{32,40},{40,32},{48,56},{56,48},{64,72... | collective-permute-start | bytes 393224 | tf_op jit(solution)/shard_map/ppermute | solution.py:428
  6.3 0.0 copy-done
  6.3 0.0 copy-done.1
  6.3 0.0 copy-done.2
  6.3 0.0 copy-done.3
  6.3 0.0 copy-done.5
  6.3 0.0 copy-done.7
  6.4 3.2 %before.1 = (bf16[3456,256]{1,0:T(8,128)(2,1)S(1)}, bf16[3456,256]{1,0:T(8,128)(2,1)S(1)}, bf16[512,2048]{1,0:T(8,128)(2,1)S(1)}, bf16[1024,256]{1,0:T(8,128)(2,...) custom-call(f32[12582912]{0:T(1024)} %begin.1.begun, ...), custom_call_target="tpu_custom_call" | custom-call | flops 100000000 | bytes 8388608 | tf_op jit(solution)/shard_map/before/pallas_call | solution.py:172
  9.5 0.1 pad_add_fusion.where
  9.6 0.0 collective-permute-done.1.xb
  9.6 0.0 collective-permute-done.xa
  9.6 0.8 %columns.1 = (bf16[24,2048]{1,0:T(8,128)(2,1)S(1)}, bf16[24,2048]{1,0:T(8,128)(2,1)S(1)}) custom-call(s32[4]{0:T(128)S(1)} %pad_add_fusion.where, f32[48,2048]{1,0:T(8,128)S(1)} %get-tuple-element.25.mine, bf16[2,16,2048]{2,1,0:T(8,128)(2,1)S(1)} %collective-permute-done.1.xb, bf16[2,16,2048]{2,1,0:T(8,128)(2,1)S(1)} %collective-permute-done.xa), custom_call_target="tpu_custom_call" | custom-call | tf_op jit(solution)/shard_map/columns/pallas_call | solution.py:225
  10.4 1.3 %collective-permute-start.2 = (bf16[24,2048]{1,0:T(8,128)(2,1)S(1)}, bf16[24,2048]{1,0:T(8,128)(2,1)S(1)}, u32[]{:S(2)}, u32[]{:S(2)}) collective-permute-start(bf16[24,2048]{1,0:T(8,128)(2,1)S(1)} %get-tuple-element.26.near), channel_id=1, source_target_pairs={{0,1},{1,0},{2,3},{3,2},{4,5},{5,4},{6,7},{7,6},{8,9},{9,8},{10,11... | collective-permute-start | bytes 294920 | tf_op jit(solution)/shard_map/ppermute | solution.py:434
  11.7 3.4 %collective-permute-start.3 = (bf16[24,2048]{1,0:T(8,128)(2,1)S(1)}, bf16[24,2048]{1,0:T(8,128)(2,1)S(1)}, u32[]{:S(2)}, u32[]{:S(2)}) collective-permute-start(bf16[24,2048]{1,0:T(8,128)(2,1)S(1)} %get-tuple-element.27.far), channel_id=1, source_target_pairs={{1,2},{2,1},{3,4},{4,3},{5,6},{6,5},{9,10},{10,9},{11,12},{12,11},... | collective-permute-start | bytes 294920 | tf_op jit(solution)/shard_map/ppermute | solution.py:433
  15.1 2.0 %slabs.1 = (bf16[160,2176]{1,0:T(8,128)(2,1)S(1)}, bf16[160,2176]{1,0:T(8,128)(2,1)S(1)}, bf16[160,2176]{1,0:T(8,128)(2,1)S(1)}, bf16[128,2048]{1,0:T(8,128)(2,1...) custom-call(s32[4]{0:T(128)S(1)} %pad_add_fusion.where, bf16[8,16,2048]{2,1,0:T(8,128)(2,1)S(1)} %copy-done, ...), custom_call_target="tpu_custom_call" | custom-call | flops 2000000000 | bytes 1048576 | tf_op jit(solution)/shard_map/slabs/pallas_call | solution.py:269
  17.2 0.0 collective-permute-done.2.ya
  17.2 0.5 %collective-permute-done.3.yb = bf16[24,2048]{1,0:T(8,128)(2,1)S(1)} collective-permute-done((bf16[24,2048]{1,0:T(8,128)(2,1)S(1)}, bf16[24,2048]{1,0:T(8,128)(2,1)S(1)}, u32[]{:S(2)}, u32[]{:S(2)}) %collective-permute-start.3) | collective-permute-done | bytes 98336 | tf_op jit(solution)/shard_map/ppermute | solution.py:433
  17.6 2.0 %outer.1 = (bf16[160,2176]{1,0:T(8,128)(2,1)S(1)}, bf16[160,2176]{1,0:T(8,128)(2,1)S(1)}, bf16[160,2176]{1,0:T(8,128)(2,1)S(1)}, bf16[128,2048]{1,0:T(8,128)(2,1)S(1)}) custom-call(s32[4]{0:T(128)S(1)} %pad_add_fusion.where, bf16[160,2176]{1,0:T(8,128)(2,1)S(1)} %get-tuple-element.29.a0i, ...), custom_call_target="tpu_custom_call", output_to_operand_aliasing={{0}: (1, {}), {1}: (2, {}), {2}: (3, {}), {3}: (4, {})} | custom-call | tf_op jit(solution)/shard_map/outer/pallas_call | solution.py:340
  19.7 0.0 copy-start.4
  19.7 0.0 copy-start.6
  19.7 3.2 %second.1 = bf16[1024,128]{1,0:T(8,128)(2,1)S(1)} custom-call(bf16[160,2176]{1,0:T(8,128)(2,1)S(1)} %get-tuple-element.35.a0, bf16[160,2176]{1,0:T(8,128)(2,1)S(1)} %get-tuple-element.36.a1, bf16[160,2176]{1,0:T(8,128)(2,1)S(1)} %get-tuple-element.37.a2, bf16[128,2048]{1,0:T(8,128)(2,1)S(1)} %get-tuple-element.38.own, ...), custom_call_target="tpu_custom_call" | custom-call | tf_op jit(solution)/shard_map/second/pallas_call | solution.py:350
  22.9 21.4 %all_to_all.5 = bf16[128,8,128]{2,1,0:T(8,128)(2,1)S(1)} all-to-all(bf16[128,8,128]{2,1,0:T(8,128)(2,1)S(1)} %bitcast.7), channel_id=1, replica_groups=mesh['gx'=16,'gy'=8] {'gx','gy'}, dimensions={0} | all-to-all | bytes 524288 | tf_op jit(solution)/shard_map/all_to_all | solution.py:438
  44.3 0.0 copy-done.4
  44.3 0.0 copy-done.6
  44.3 1.2 %head.1 = bf16[64,128]{1,0:T(8,128)(2,1)} custom-call(bf16[1024,128]{1,0:T(8,128)(2,1)S(1)} %bitcast.8, bf16[64,256]{1,0:T(8,128)(2,1)S(1)} %copy-done.6, bf16[256,128]{1,0:T(8,128)(2,1)S(1)} %copy-done.4), custom_call_target="tpu_custom_call" | custom-call | tf_op jit(solution)/shard_map/head/pallas_call | solution.py:401
  (1 shorter events, 0.0 us)
Async XLA Ops:
  1.0 8.6 %collective-permute-start.1 = (bf16[2,16,2048]{2,1,0:T(8,128)(2,1)S(1)}, bf16[2,16,2048]{2,1,0:T(8,128)(2,1)S(1)}, u32[]{:S(2)}, u32[]{:S(2)}) collective-permute-start(bf16[2,16,2048]{2,1,0:T(8,128)(2,1)S(1)} %get-tuple-element.43), channel_id=1, source_target_pairs={{8,16},{16,8},{24,32},{32,24},{40,48},{48,40},{56,64},{64,56},{72,... | collective-permute-start | bytes 393224 | tf_op jit(solution)/shard_map/ppermute | solution.py:427
  1.7 4.6 %copy-start = (bf16[8,16,2048]{2,1,0:T(8,128)(2,1)S(1)}, bf16[8,16,2048]{2,1,0:T(8,128)(2,1)}, u32[]{:S(2)}) copy-start(bf16[8,16,2048]{2,1,0:T(8,128)(2,1)} %v.3) | copy-start | bytes 1572868
  1.7 4.6 %copy-start.1 = (bf16[1728,64]{0,1:T(8,128)(2,1)S(1)}, bf16[1728,64]{0,1:T(8,128)(2,1)}, u32[]{:S(2)}) copy-start(bf16[1728,64]{0,1:T(8,128)(2,1)} %param.12) | copy-start | bytes 663556
  1.7 4.6 %copy-start.2 = (bf16[1728,64]{0,1:T(8,128)(2,1)S(1)}, bf16[1728,64]{0,1:T(8,128)(2,1)}, u32[]{:S(2)}) copy-start(bf16[1728,64]{0,1:T(8,128)(2,1)} %param.13) | copy-start | bytes 663556
  1.7 4.6 %copy-start.3 = (s32[8,16,32]{2,1,0:T(8,128)S(1)}, s32[8,16,32]{2,1,0:T(8,128)}, u32[]{:S(2)}) copy-start(s32[8,16,32]{2,1,0:T(8,128)} %labels.1) | copy-start | bytes 49156
  1.7 4.6 %copy-start.5 = (s32[8192]{0:T(1024)S(1)}, s32[8192]{0:T(1024)}, u32[]{:S(2)}) copy-start(s32[8192]{0:T(1024)} %param.11) | copy-start | bytes 98308
  1.7 4.6 %copy-start.7 = (s32[1,256]{1,0:T(1,128)S(1)}, s32[1,256]{1,0:T(1,128)}, u32[]{:S(2)}) copy-start(s32[1,256]{1,0:T(1,128)} %lists.1) | copy-start | bytes 3076
  1.7 7.9 %collective-permute-start = (bf16[2,16,2048]{2,1,0:T(8,128)(2,1)S(1)}, bf16[2,16,2048]{2,1,0:T(8,128)(2,1)S(1)}, u32[]{:S(2)}, u32[]{:S(2)}) collective-permute-start(bf16[2,16,2048]{2,1,0:T(8,128)(2,1)S(1)} %get-tuple-element.44), channel_id=1, source_target_pairs={{0,8},{8,0},{16,24},{24,16},{32,40},{40,32},{48,56},{56,48},{64,72... | collective-permute-start | bytes 393224 | tf_op jit(solution)/shard_map/ppermute | solution.py:428
  10.4 6.8 %collective-permute-start.2 = (bf16[24,2048]{1,0:T(8,128)(2,1)S(1)}, bf16[24,2048]{1,0:T(8,128)(2,1)S(1)}, u32[]{:S(2)}, u32[]{:S(2)}) collective-permute-start(bf16[24,2048]{1,0:T(8,128)(2,1)S(1)} %get-tuple-element.26.near), channel_id=1, source_target_pairs={{0,1},{1,0},{2,3},{3,2},{4,5},{5,4},{6,7},{7,6},{8,9},{9,8},{10,11... | collective-permute-start | bytes 294920 | tf_op jit(solution)/shard_map/ppermute | solution.py:434
  11.7 5.9 %collective-permute-start.3 = (bf16[24,2048]{1,0:T(8,128)(2,1)S(1)}, bf16[24,2048]{1,0:T(8,128)(2,1)S(1)}, u32[]{:S(2)}, u32[]{:S(2)}) collective-permute-start(bf16[24,2048]{1,0:T(8,128)(2,1)S(1)} %get-tuple-element.27.far), channel_id=1, source_target_pairs={{1,2},{2,1},{3,4},{4,3},{5,6},{6,5},{9,10},{10,9},{11,12},{12,11},... | collective-permute-start | bytes 294920 | tf_op jit(solution)/shard_map/ppermute | solution.py:433
  19.7 24.7 %copy-start.4 = (bf16[256,128]{1,0:T(8,128)(2,1)S(1)}, bf16[256,128]{1,0:T(8,128)(2,1)}, u32[]{:S(2)}) copy-start(bf16[256,128]{1,0:T(8,128)(2,1)} %w_out.1) | copy-start | bytes 196612
  19.7 24.6 %copy-start.6 = (bf16[64,256]{1,0:T(8,128)(2,1)S(1)}, bf16[64,256]{1,0:T(8,128)(2,1)}, u32[]{:S(2)}) copy-start(bf16[64,256]{1,0:T(8,128)(2,1)} %w_in.1) | copy-start | bytes 98308

commit v6 on v5

--- a/solution.py
+++ b/solution.py
@@ -377,7 +377,10 @@
     lanes = iota((slots, 128), 1)
     sums = both[0:slots] + pltpu.roll(both[slots : 2 * slots], 64, 1)
     rows = jnp.where(lanes < CH, sums, meta[...].astype(F32)).astype(BF16)
-    out[...] = dot(place[...], rows).astype(BF16)
+    step = place.shape[0] // 4
+    for k in range(4):
+        at = k * step
+        out[at : at + step] = dot(place[at : at + step], rows).astype(BF16)
 
 
 def head_kernel(got, w_in, w_out, out):

time: 45.7 us -> 45.8 us (level)
  no operation moved by 1% of the time
where the time goes in v6:
time: 45.8 us; the launch traced here: 45.6 us
  blocking collectives  21.4 us (47%)
  Pallas kernels  12.5 us (27%)
  starting transfers between devices  10 us (22%)
  local copies, waits for them, and re-layouts  1.04 us (2%)
  waiting for transfers between devices  0.46 us (1%)
    all_to_all x1, blocking collectives, local(): got = lax.all_to_all(rows, ('gx', 'gy'), 0, 0, tiled=True)  21.4 us
    ppermute x1, starting transfers between devices, local(): xa = lax.ppermute(to_a, 'gx', inner_x)  4.57 us
    ppermute x1, starting transfers between devices, local(): yb = lax.ppermute(far, 'gy', outer_y)  3.43 us
    pallas_call x1, Pallas kernels, outer(): pl.pallas_call(second_kernel, out_shape=jax.ShapeDtypeStruct((place.shape...  3.26 us
    pallas_call x1, Pallas kernels, before(): pl.pallas_call(before_kernel, out_shape=(jax.ShapeDtypeStruct((3456, 256)...  3.16 us
    pallas_call x1, Pallas kernels, outer(): pl.pallas_call(outer_kernel, out_shape=(full, full, full, jax.ShapeDtypeS...  2.03 us
    pallas_call x1, Pallas kernels, slabs(): pl.pallas_call(slabs_kernel, out_shape=(full, full, full, jax.ShapeDtypeS...  2.01 us
    ppermute x1, starting transfers between devices, local(): ya = lax.ppermute(near, 'gy', inner_y)  1.33 us
  transfers between devices with their start and end apart: 4, of which 1 were waited for; matrix products, arithmetic and copies ran while one was open for 0% of the time, Pallas kernels for 11%

profile of v6, /device:TPU:1, one launch (start us, length us, event | category | flops | bytes accessed | tf_op | source)
XLA Modules:
  0.0 45.6 jit_solution(2315790418652906189)
XLA Ops:
  0.0 1.0 %constant_dynamic-slice_fusion = (bf16[2,16,2048]{2,1,0:T(8,128)(2,1)S(1)}, bf16[2,16,2048]{2,1,0:T(8,128)(2,1)S(1)}) fusion(bf16[8,16,2048]{2,1,0:T(8,128)(2,1)} %v.3, s32[]{:T(128)S(6)} %select_n.18, s32[]{:T(128)S(6)} %select_n.17), kind=kLoop, calls=%fused_computation.1 | loop fusion | bytes 524296 | tf_op jit(solution)/shard_map/dynamic_slice | solution.py:427
  1.0 0.7 %collective-permute-start.1 = (bf16[2,16,2048]{2,1,0:T(8,128)(2,1)S(1)}, bf16[2,16,2048]{2,1,0:T(8,128)(2,1)S(1)}, u32[]{:S(2)}, u32[]{:S(2)}) collective-permute-start(bf16[2,16,2048]{2,1,0:T(8,128)(2,1)S(1)} %get-tuple-element.43), channel_id=1, source_target_pairs={{8,16},{16,8},{24,32},{32,24},{40,48},{48,40},{56,64},{64,56},{72,... | collective-permute-start | bytes 393224 | tf_op jit(solution)/shard_map/ppermute | solution.py:430
  1.7 0.0 copy-start
  1.7 0.0 copy-start.1
  1.7 0.0 copy-start.2
  1.7 0.0 copy-start.3
  1.7 0.0 copy-start.5
  1.7 0.0 copy-start.7
  1.7 4.6 %collective-permute-start = (bf16[2,16,2048]{2,1,0:T(8,128)(2,1)S(1)}, bf16[2,16,2048]{2,1,0:T(8,128)(2,1)S(1)}, u32[]{:S(2)}, u32[]{:S(2)}) collective-permute-start(bf16[2,16,2048]{2,1,0:T(8,128)(2,1)S(1)} %get-tuple-element.44), channel_id=1, source_target_pairs={{0,8},{8,0},{16,24},{24,16},{32,40},{40,32},{48,56},{56,48},{64,72... | collective-permute-start | bytes 393224 | tf_op jit(solution)/shard_map/ppermute | solution.py:431
  6.3 0.0 copy-done
  6.3 0.0 copy-done.1
  6.3 0.0 copy-done.2
  6.3 0.0 copy-done.3
  6.3 0.0 copy-done.5
  6.3 0.0 copy-done.7
  6.4 3.2 %before.1 = (bf16[3456,256]{1,0:T(8,128)(2,1)S(1)}, bf16[3456,256]{1,0:T(8,128)(2,1)S(1)}, bf16[512,2048]{1,0:T(8,128)(2,1)S(1)}, bf16[1024,256]{1,0:T(8,128)(2,...) custom-call(f32[12582912]{0:T(1024)} %begin.1.begun, ...), custom_call_target="tpu_custom_call" | custom-call | flops 100000000 | bytes 8388608 | tf_op jit(solution)/shard_map/before/pallas_call | solution.py:172
  9.5 0.1 pad_add_fusion.where
  9.6 0.0 collective-permute-done.1.xb
  9.6 0.0 collective-permute-done.xa
  9.6 0.8 %columns.1 = (bf16[24,2048]{1,0:T(8,128)(2,1)S(1)}, bf16[24,2048]{1,0:T(8,128)(2,1)S(1)}) custom-call(s32[4]{0:T(128)S(1)} %pad_add_fusion.where, f32[48,2048]{1,0:T(8,128)S(1)} %get-tuple-element.25.mine, bf16[2,16,2048]{2,1,0:T(8,128)(2,1)S(1)} %collective-permute-done.1.xb, bf16[2,16,2048]{2,1,0:T(8,128)(2,1)S(1)} %collective-permute-done.xa), custom_call_target="tpu_custom_call" | custom-call | tf_op jit(solution)/shard_map/columns/pallas_call | solution.py:225
  10.4 1.3 %collective-permute-start.2 = (bf16[24,2048]{1,0:T(8,128)(2,1)S(1)}, bf16[24,2048]{1,0:T(8,128)(2,1)S(1)}, u32[]{:S(2)}, u32[]{:S(2)}) collective-permute-start(bf16[24,2048]{1,0:T(8,128)(2,1)S(1)} %get-tuple-element.26.near), channel_id=1, source_target_pairs={{0,1},{1,0},{2,3},{3,2},{4,5},{5,4},{6,7},{7,6},{8,9},{9,8},{10,11... | collective-permute-start | bytes 294920 | tf_op jit(solution)/shard_map/ppermute | solution.py:437
  11.7 3.4 %collective-permute-start.3 = (bf16[24,2048]{1,0:T(8,128)(2,1)S(1)}, bf16[24,2048]{1,0:T(8,128)(2,1)S(1)}, u32[]{:S(2)}, u32[]{:S(2)}) collective-permute-start(bf16[24,2048]{1,0:T(8,128)(2,1)S(1)} %get-tuple-element.27.far), channel_id=1, source_target_pairs={{1,2},{2,1},{3,4},{4,3},{5,6},{6,5},{9,10},{10,9},{11,12},{12,11},... | collective-permute-start | bytes 294920 | tf_op jit(solution)/shard_map/ppermute | solution.py:436
  15.1 2.0 %slabs.1 = (bf16[160,2176]{1,0:T(8,128)(2,1)S(1)}, bf16[160,2176]{1,0:T(8,128)(2,1)S(1)}, bf16[160,2176]{1,0:T(8,128)(2,1)S(1)}, bf16[128,2048]{1,0:T(8,128)(2,1...) custom-call(s32[4]{0:T(128)S(1)} %pad_add_fusion.where, bf16[8,16,2048]{2,1,0:T(8,128)(2,1)S(1)} %copy-done, ...), custom_call_target="tpu_custom_call" | custom-call | flops 2000000000 | bytes 1048576 | tf_op jit(solution)/shard_map/slabs/pallas_call | solution.py:269
  17.2 0.0 collective-permute-done.2.ya
  17.2 0.5 %collective-permute-done.3.yb = bf16[24,2048]{1,0:T(8,128)(2,1)S(1)} collective-permute-done((bf16[24,2048]{1,0:T(8,128)(2,1)S(1)}, bf16[24,2048]{1,0:T(8,128)(2,1)S(1)}, u32[]{:S(2)}, u32[]{:S(2)}) %collective-permute-start.3) | collective-permute-done | bytes 98336 | tf_op jit(solution)/shard_map/ppermute | solution.py:436
  17.6 2.0 %outer.1 = (bf16[160,2176]{1,0:T(8,128)(2,1)S(1)}, bf16[160,2176]{1,0:T(8,128)(2,1)S(1)}, bf16[160,2176]{1,0:T(8,128)(2,1)S(1)}, bf16[128,2048]{1,0:T(8,128)(2,1)S(1)}) custom-call(s32[4]{0:T(128)S(1)} %pad_add_fusion.where, bf16[160,2176]{1,0:T(8,128)(2,1)S(1)} %get-tuple-element.29.a0i, ...), custom_call_target="tpu_custom_call", output_to_operand_aliasing={{0}: (1, {}), {1}: (2, {}), {2}: (3, {}), {3}: (4, {})} | custom-call | tf_op jit(solution)/shard_map/outer/pallas_call | solution.py:340
  19.7 0.0 copy-start.4
  19.7 0.0 copy-start.6
  19.7 3.3 %second.1 = bf16[1024,128]{1,0:T(8,128)(2,1)S(1)} custom-call(bf16[160,2176]{1,0:T(8,128)(2,1)S(1)} %get-tuple-element.35.a0, bf16[160,2176]{1,0:T(8,128)(2,1)S(1)} %get-tuple-element.36.a1, bf16[160,2176]{1,0:T(8,128)(2,1)S(1)} %get-tuple-element.37.a2, bf16[128,2048]{1,0:T(8,128)(2,1)S(1)} %get-tuple-element.38.own, ...), custom_call_target="tpu_custom_call" | custom-call | tf_op jit(solution)/shard_map/second/pallas_call | solution.py:350
  23.0 21.4 %all_to_all.5 = bf16[128,8,128]{2,1,0:T(8,128)(2,1)S(1)} all-to-all(bf16[128,8,128]{2,1,0:T(8,128)(2,1)S(1)} %bitcast.7), channel_id=1, replica_groups=mesh['gx'=16,'gy'=8] {'gx','gy'}, dimensions={0} | all-to-all | bytes 524288 | tf_op jit(solution)/shard_map/all_to_all | solution.py:441
  44.3 0.0 copy-done.4
  44.3 0.0 copy-done.6
  44.3 1.2 %head.1 = bf16[64,128]{1,0:T(8,128)(2,1)} custom-call(bf16[1024,128]{1,0:T(8,128)(2,1)S(1)} %bitcast.8, bf16[64,256]{1,0:T(8,128)(2,1)S(1)} %copy-done.6, bf16[256,128]{1,0:T(8,128)(2,1)S(1)} %copy-done.4), custom_call_target="tpu_custom_call" | custom-call | tf_op jit(solution)/shard_map/head/pallas_call | solution.py:404
  (1 shorter events, 0.0 us)
Async XLA Ops:
  1.0 8.6 %collective-permute-start.1 = (bf16[2,16,2048]{2,1,0:T(8,128)(2,1)S(1)}, bf16[2,16,2048]{2,1,0:T(8,128)(2,1)S(1)}, u32[]{:S(2)}, u32[]{:S(2)}) collective-permute-start(bf16[2,16,2048]{2,1,0:T(8,128)(2,1)S(1)} %get-tuple-element.43), channel_id=1, source_target_pairs={{8,16},{16,8},{24,32},{32,24},{40,48},{48,40},{56,64},{64,56},{72,... | collective-permute-start | bytes 393224 | tf_op jit(solution)/shard_map/ppermute | solution.py:430
  1.7 4.6 %copy-start = (bf16[8,16,2048]{2,1,0:T(8,128)(2,1)S(1)}, bf16[8,16,2048]{2,1,0:T(8,128)(2,1)}, u32[]{:S(2)}) copy-start(bf16[8,16,2048]{2,1,0:T(8,128)(2,1)} %v.3) | copy-start | bytes 1572868
  1.7 4.6 %copy-start.1 = (bf16[1728,64]{0,1:T(8,128)(2,1)S(1)}, bf16[1728,64]{0,1:T(8,128)(2,1)}, u32[]{:S(2)}) copy-start(bf16[1728,64]{0,1:T(8,128)(2,1)} %param.12) | copy-start | bytes 663556
  1.7 4.6 %copy-start.2 = (bf16[1728,64]{0,1:T(8,128)(2,1)S(1)}, bf16[1728,64]{0,1:T(8,128)(2,1)}, u32[]{:S(2)}) copy-start(bf16[1728,64]{0,1:T(8,128)(2,1)} %param.13) | copy-start | bytes 663556
  1.7 4.6 %copy-start.3 = (s32[8,16,32]{2,1,0:T(8,128)S(1)}, s32[8,16,32]{2,1,0:T(8,128)}, u32[]{:S(2)}) copy-start(s32[8,16,32]{2,1,0:T(8,128)} %labels.1) | copy-start | bytes 49156
  1.7 4.6 %copy-start.5 = (s32[8192]{0:T(1024)S(1)}, s32[8192]{0:T(1024)}, u32[]{:S(2)}) copy-start(s32[8192]{0:T(1024)} %param.11) | copy-start | bytes 98308
  1.7 4.6 %copy-start.7 = (s32[1,256]{1,0:T(1,128)S(1)}, s32[1,256]{1,0:T(1,128)}, u32[]{:S(2)}) copy-start(s32[1,256]{1,0:T(1,128)} %lists.1) | copy-start | bytes 3076
  1.7 7.9 %collective-permute-start = (bf16[2,16,2048]{2,1,0:T(8,128)(2,1)S(1)}, bf16[2,16,2048]{2,1,0:T(8,128)(2,1)S(1)}, u32[]{:S(2)}, u32[]{:S(2)}) collective-permute-start(bf16[2,16,2048]{2,1,0:T(8,128)(2,1)S(1)} %get-tuple-element.44), channel_id=1, source_target_pairs={{0,8},{8,0},{16,24},{24,16},{32,40},{40,32},{48,56},{56,48},{64,72... | collective-permute-start | bytes 393224 | tf_op jit(solution)/shard_map/ppermute | solution.py:431
  10.4 6.8 %collective-permute-start.2 = (bf16[24,2048]{1,0:T(8,128)(2,1)S(1)}, bf16[24,2048]{1,0:T(8,128)(2,1)S(1)}, u32[]{:S(2)}, u32[]{:S(2)}) collective-permute-start(bf16[24,2048]{1,0:T(8,128)(2,1)S(1)} %get-tuple-element.26.near), channel_id=1, source_target_pairs={{0,1},{1,0},{2,3},{3,2},{4,5},{5,4},{6,7},{7,6},{8,9},{9,8},{10,11... | collective-permute-start | bytes 294920 | tf_op jit(solution)/shard_map/ppermute | solution.py:437
  11.7 5.9 %collective-permute-start.3 = (bf16[24,2048]{1,0:T(8,128)(2,1)S(1)}, bf16[24,2048]{1,0:T(8,128)(2,1)S(1)}, u32[]{:S(2)}, u32[]{:S(2)}) collective-permute-start(bf16[24,2048]{1,0:T(8,128)(2,1)S(1)} %get-tuple-element.27.far), channel_id=1, source_target_pairs={{1,2},{2,1},{3,4},{4,3},{5,6},{6,5},{9,10},{10,9},{11,12},{12,11},... | collective-permute-start | bytes 294920 | tf_op jit(solution)/shard_map/ppermute | solution.py:436
  19.7 24.7 %copy-start.4 = (bf16[256,128]{1,0:T(8,128)(2,1)S(1)}, bf16[256,128]{1,0:T(8,128)(2,1)}, u32[]{:S(2)}) copy-start(bf16[256,128]{1,0:T(8,128)(2,1)} %w_out.1) | copy-start | bytes 196612
  19.7 24.7 %copy-start.6 = (bf16[64,256]{1,0:T(8,128)(2,1)S(1)}, bf16[64,256]{1,0:T(8,128)(2,1)}, u32[]{:S(2)}) copy-start(bf16[64,256]{1,0:T(8,128)(2,1)} %w_in.1) | copy-start | bytes 98308

commit v7 on v6

--- a/solution.py
+++ b/solution.py
@@ -373,9 +373,10 @@
         second = dot(left, wb2[...]) + own[:, at : at + 256].astype(F32)
         fresh[at : at + 128] = second[:, 0:128].astype(BF16)
         fresh[at + 128 : at + 256] = second[:, 128:256].astype(BF16)
-    both = dot(member[...], fresh[...])
+    odd = dot(member[slots : 2 * slots], fresh[...])
+    even = dot(member[0:slots], fresh[...])
     lanes = iota((slots, 128), 1)
-    sums = both[0:slots] + pltpu.roll(both[slots : 2 * slots], 64, 1)
+    sums = even + pltpu.roll(odd, 64, 1)
     rows = jnp.where(lanes < CH, sums, meta[...].astype(F32)).astype(BF16)
     step = place.shape[0] // 4
     for k in range(4):

time: 45.8 us -> 45.4 us (level)
  no operation moved by 1% of the time
where the time goes in v7:
time: 45.4 us; the launch traced here: 45.2 us
  blocking collectives  21.4 us (47%)
  Pallas kernels  12.1 us (27%)
  starting transfers between devices  10 us (22%)
  local copies, waits for them, and re-layouts  1.04 us (2%)
  waiting for transfers between devices  0.46 us (1%)
    all_to_all x1, blocking collectives, local(): got = lax.all_to_all(rows, ('gx', 'gy'), 0, 0, tiled=True)  21.4 us
    ppermute x1, starting transfers between devices, local(): xa = lax.ppermute(to_a, 'gx', inner_x)  4.57 us
    ppermute x1, starting transfers between devices, local(): yb = lax.ppermute(far, 'gy', outer_y)  3.43 us
    pallas_call x1, Pallas kernels, before(): pl.pallas_call(before_kernel, out_shape=(jax.ShapeDtypeStruct((3456, 256)...  3.16 us
    pallas_call x1, Pallas kernels, outer(): pl.pallas_call(second_kernel, out_shape=jax.ShapeDtypeStruct((place.shape...  2.92 us
    pallas_call x1, Pallas kernels, outer(): pl.pallas_call(outer_kernel, out_shape=(full, full, full, jax.ShapeDtypeS...  2.03 us
    pallas_call x1, Pallas kernels, slabs(): pl.pallas_call(slabs_kernel, out_shape=(full, full, full, jax.ShapeDtypeS...  2.01 us
    ppermute x1, starting transfers between devices, local(): ya = lax.ppermute(near, 'gy', inner_y)  1.33 us
  transfers between devices with their start and end apart: 4, of which 1 were waited for; matrix products, arithmetic and copies ran while one was open for 0% of the time, Pallas kernels for 11%

profile of v7, /device:TPU:1, one launch (start us, length us, event | category | flops | bytes accessed | tf_op | source)
XLA Modules:
  0.0 45.2 jit_solution(16645419099619963148)
XLA Ops:
  0.0 1.0 %constant_dynamic-slice_fusion = (bf16[2,16,2048]{2,1,0:T(8,128)(2,1)S(1)}, bf16[2,16,2048]{2,1,0:T(8,128)(2,1)S(1)}) fusion(bf16[8,16,2048]{2,1,0:T(8,128)(2,1)} %v.3, s32[]{:T(128)S(6)} %select_n.18, s32[]{:T(128)S(6)} %select_n.17), kind=kLoop, calls=%fused_computation.1 | loop fusion | bytes 524296 | tf_op jit(solution)/shard_map/dynamic_slice | solution.py:428
  1.0 0.7 %collective-permute-start.1 = (bf16[2,16,2048]{2,1,0:T(8,128)(2,1)S(1)}, bf16[2,16,2048]{2,1,0:T(8,128)(2,1)S(1)}, u32[]{:S(2)}, u32[]{:S(2)}) collective-permute-start(bf16[2,16,2048]{2,1,0:T(8,128)(2,1)S(1)} %get-tuple-element.43), channel_id=1, source_target_pairs={{8,16},{16,8},{24,32},{32,24},{40,48},{48,40},{56,64},{64,56},{72,... | collective-permute-start | bytes 393224 | tf_op jit(solution)/shard_map/ppermute | solution.py:431
  1.7 0.0 copy-start
  1.7 0.0 copy-start.1
  1.7 0.0 copy-start.2
  1.7 0.0 copy-start.3
  1.7 0.0 copy-start.5
  1.7 0.0 copy-start.7
  1.7 4.6 %collective-permute-start = (bf16[2,16,2048]{2,1,0:T(8,128)(2,1)S(1)}, bf16[2,16,2048]{2,1,0:T(8,128)(2,1)S(1)}, u32[]{:S(2)}, u32[]{:S(2)}) collective-permute-start(bf16[2,16,2048]{2,1,0:T(8,128)(2,1)S(1)} %get-tuple-element.44), channel_id=1, source_target_pairs={{0,8},{8,0},{16,24},{24,16},{32,40},{40,32},{48,56},{56,48},{64,72... | collective-permute-start | bytes 393224 | tf_op jit(solution)/shard_map/ppermute | solution.py:432
  6.3 0.0 copy-done
  6.3 0.0 copy-done.1
  6.3 0.0 copy-done.2
  6.3 0.0 copy-done.3
  6.3 0.0 copy-done.5
  6.3 0.0 copy-done.7
  6.4 3.2 %before.1 = (bf16[3456,256]{1,0:T(8,128)(2,1)S(1)}, bf16[3456,256]{1,0:T(8,128)(2,1)S(1)}, bf16[512,2048]{1,0:T(8,128)(2,1)S(1)}, bf16[1024,256]{1,0:T(8,128)(2,...) custom-call(f32[12582912]{0:T(1024)} %begin.1.begun, ...), custom_call_target="tpu_custom_call" | custom-call | flops 100000000 | bytes 8388608 | tf_op jit(solution)/shard_map/before/pallas_call | solution.py:172
  9.5 0.1 pad_add_fusion.where
  9.6 0.0 collective-permute-done.1.xb
  9.6 0.0 collective-permute-done.xa
  9.6 0.8 %columns.1 = (bf16[24,2048]{1,0:T(8,128)(2,1)S(1)}, bf16[24,2048]{1,0:T(8,128)(2,1)S(1)}) custom-call(s32[4]{0:T(128)S(1)} %pad_add_fusion.where, f32[48,2048]{1,0:T(8,128)S(1)} %get-tuple-element.25.mine, bf16[2,16,2048]{2,1,0:T(8,128)(2,1)S(1)} %collective-permute-done.1.xb, bf16[2,16,2048]{2,1,0:T(8,128)(2,1)S(1)} %collective-permute-done.xa), custom_call_target="tpu_custom_call" | custom-call | tf_op jit(solution)/shard_map/columns/pallas_call | solution.py:225
  10.4 1.3 %collective-permute-start.2 = (bf16[24,2048]{1,0:T(8,128)(2,1)S(1)}, bf16[24,2048]{1,0:T(8,128)(2,1)S(1)}, u32[]{:S(2)}, u32[]{:S(2)}) collective-permute-start(bf16[24,2048]{1,0:T(8,128)(2,1)S(1)} %get-tuple-element.26.near), channel_id=1, source_target_pairs={{0,1},{1,0},{2,3},{3,2},{4,5},{5,4},{6,7},{7,6},{8,9},{9,8},{10,11... | collective-permute-start | bytes 294920 | tf_op jit(solution)/shard_map/ppermute | solution.py:438
  11.7 3.4 %collective-permute-start.3 = (bf16[24,2048]{1,0:T(8,128)(2,1)S(1)}, bf16[24,2048]{1,0:T(8,128)(2,1)S(1)}, u32[]{:S(2)}, u32[]{:S(2)}) collective-permute-start(bf16[24,2048]{1,0:T(8,128)(2,1)S(1)} %get-tuple-element.27.far), channel_id=1, source_target_pairs={{1,2},{2,1},{3,4},{4,3},{5,6},{6,5},{9,10},{10,9},{11,12},{12,11},... | collective-permute-start | bytes 294920 | tf_op jit(solution)/shard_map/ppermute | solution.py:437
  15.1 2.0 %slabs.1 = (bf16[160,2176]{1,0:T(8,128)(2,1)S(1)}, bf16[160,2176]{1,0:T(8,128)(2,1)S(1)}, bf16[160,2176]{1,0:T(8,128)(2,1)S(1)}, bf16[128,2048]{1,0:T(8,128)(2,1...) custom-call(s32[4]{0:T(128)S(1)} %pad_add_fusion.where, bf16[8,16,2048]{2,1,0:T(8,128)(2,1)S(1)} %copy-done, ...), custom_call_target="tpu_custom_call" | custom-call | flops 2000000000 | bytes 1048576 | tf_op jit(solution)/shard_map/slabs/pallas_call | solution.py:269
  17.2 0.0 collective-permute-done.2.ya
  17.2 0.5 %collective-permute-done.3.yb = bf16[24,2048]{1,0:T(8,128)(2,1)S(1)} collective-permute-done((bf16[24,2048]{1,0:T(8,128)(2,1)S(1)}, bf16[24,2048]{1,0:T(8,128)(2,1)S(1)}, u32[]{:S(2)}, u32[]{:S(2)}) %collective-permute-start.3) | collective-permute-done | bytes 98336 | tf_op jit(solution)/shard_map/ppermute | solution.py:437
  17.6 2.0 %outer.1 = (bf16[160,2176]{1,0:T(8,128)(2,1)S(1)}, bf16[160,2176]{1,0:T(8,128)(2,1)S(1)}, bf16[160,2176]{1,0:T(8,128)(2,1)S(1)}, bf16[128,2048]{1,0:T(8,128)(2,1)S(1)}) custom-call(s32[4]{0:T(128)S(1)} %pad_add_fusion.where, bf16[160,2176]{1,0:T(8,128)(2,1)S(1)} %get-tuple-element.29.a0i, ...), custom_call_target="tpu_custom_call", output_to_operand_aliasing={{0}: (1, {}), {1}: (2, {}), {2}: (3, {}), {3}: (4, {})} | custom-call | tf_op jit(solution)/shard_map/outer/pallas_call | solution.py:340
  19.7 0.0 copy-start.4
  19.7 0.0 copy-start.6
  19.7 2.9 %second.1 = bf16[1024,128]{1,0:T(8,128)(2,1)S(1)} custom-call(bf16[160,2176]{1,0:T(8,128)(2,1)S(1)} %get-tuple-element.35.a0, bf16[160,2176]{1,0:T(8,128)(2,1)S(1)} %get-tuple-element.36.a1, bf16[160,2176]{1,0:T(8,128)(2,1)S(1)} %get-tuple-element.37.a2, bf16[128,2048]{1,0:T(8,128)(2,1)S(1)} %get-tuple-element.38.own, ...), custom_call_target="tpu_custom_call" | custom-call | tf_op jit(solution)/shard_map/second/pallas_call | solution.py:350
  22.6 21.4 %all_to_all.5 = bf16[128,8,128]{2,1,0:T(8,128)(2,1)S(1)} all-to-all(bf16[128,8,128]{2,1,0:T(8,128)(2,1)S(1)} %bitcast.7), channel_id=1, replica_groups=mesh['gx'=16,'gy'=8] {'gx','gy'}, dimensions={0} | all-to-all | bytes 524288 | tf_op jit(solution)/shard_map/all_to_all | solution.py:442
  44.0 0.0 copy-done.4
  44.0 0.0 copy-done.6
  44.0 1.2 %head.1 = bf16[64,128]{1,0:T(8,128)(2,1)} custom-call(bf16[1024,128]{1,0:T(8,128)(2,1)S(1)} %bitcast.8, bf16[64,256]{1,0:T(8,128)(2,1)S(1)} %copy-done.6, bf16[256,128]{1,0:T(8,128)(2,1)S(1)} %copy-done.4), custom_call_target="tpu_custom_call" | custom-call | tf_op jit(solution)/shard_map/head/pallas_call | solution.py:405
  (1 shorter events, 0.0 us)
Async XLA Ops:
  1.0 8.6 %collective-permute-start.1 = (bf16[2,16,2048]{2,1,0:T(8,128)(2,1)S(1)}, bf16[2,16,2048]{2,1,0:T(8,128)(2,1)S(1)}, u32[]{:S(2)}, u32[]{:S(2)}) collective-permute-start(bf16[2,16,2048]{2,1,0:T(8,128)(2,1)S(1)} %get-tuple-element.43), channel_id=1, source_target_pairs={{8,16},{16,8},{24,32},{32,24},{40,48},{48,40},{56,64},{64,56},{72,... | collective-permute-start | bytes 393224 | tf_op jit(solution)/shard_map/ppermute | solution.py:431
  1.7 4.6 %copy-start = (bf16[8,16,2048]{2,1,0:T(8,128)(2,1)S(1)}, bf16[8,16,2048]{2,1,0:T(8,128)(2,1)}, u32[]{:S(2)}) copy-start(bf16[8,16,2048]{2,1,0:T(8,128)(2,1)} %v.3) | copy-start | bytes 1572868
  1.7 4.6 %copy-start.1 = (bf16[1728,64]{0,1:T(8,128)(2,1)S(1)}, bf16[1728,64]{0,1:T(8,128)(2,1)}, u32[]{:S(2)}) copy-start(bf16[1728,64]{0,1:T(8,128)(2,1)} %param.12) | copy-start | bytes 663556
  1.7 4.6 %copy-start.2 = (bf16[1728,64]{0,1:T(8,128)(2,1)S(1)}, bf16[1728,64]{0,1:T(8,128)(2,1)}, u32[]{:S(2)}) copy-start(bf16[1728,64]{0,1:T(8,128)(2,1)} %param.13) | copy-start | bytes 663556
  1.7 4.6 %copy-start.3 = (s32[8,16,32]{2,1,0:T(8,128)S(1)}, s32[8,16,32]{2,1,0:T(8,128)}, u32[]{:S(2)}) copy-start(s32[8,16,32]{2,1,0:T(8,128)} %labels.1) | copy-start | bytes 49156
  1.7 4.6 %copy-start.5 = (s32[8192]{0:T(1024)S(1)}, s32[8192]{0:T(1024)}, u32[]{:S(2)}) copy-start(s32[8192]{0:T(1024)} %param.11) | copy-start | bytes 98308
  1.7 4.6 %copy-start.7 = (s32[1,256]{1,0:T(1,128)S(1)}, s32[1,256]{1,0:T(1,128)}, u32[]{:S(2)}) copy-start(s32[1,256]{1,0:T(1,128)} %lists.1) | copy-start | bytes 3076
  1.7 7.9 %collective-permute-start = (bf16[2,16,2048]{2,1,0:T(8,128)(2,1)S(1)}, bf16[2,16,2048]{2,1,0:T(8,128)(2,1)S(1)}, u32[]{:S(2)}, u32[]{:S(2)}) collective-permute-start(bf16[2,16,2048]{2,1,0:T(8,128)(2,1)S(1)} %get-tuple-element.44), channel_id=1, source_target_pairs={{0,8},{8,0},{16,24},{24,16},{32,40},{40,32},{48,56},{56,48},{64,72... | collective-permute-start | bytes 393224 | tf_op jit(solution)/shard_map/ppermute | solution.py:432
  10.4 6.8 %collective-permute-start.2 = (bf16[24,2048]{1,0:T(8,128)(2,1)S(1)}, bf16[24,2048]{1,0:T(8,128)(2,1)S(1)}, u32[]{:S(2)}, u32[]{:S(2)}) collective-permute-start(bf16[24,2048]{1,0:T(8,128)(2,1)S(1)} %get-tuple-element.26.near), channel_id=1, source_target_pairs={{0,1},{1,0},{2,3},{3,2},{4,5},{5,4},{6,7},{7,6},{8,9},{9,8},{10,11... | collective-permute-start | bytes 294920 | tf_op jit(solution)/shard_map/ppermute | solution.py:438
  11.7 5.9 %collective-permute-start.3 = (bf16[24,2048]{1,0:T(8,128)(2,1)S(1)}, bf16[24,2048]{1,0:T(8,128)(2,1)S(1)}, u32[]{:S(2)}, u32[]{:S(2)}) collective-permute-start(bf16[24,2048]{1,0:T(8,128)(2,1)S(1)} %get-tuple-element.27.far), channel_id=1, source_target_pairs={{1,2},{2,1},{3,4},{4,3},{5,6},{6,5},{9,10},{10,9},{11,12},{12,11},... | collective-permute-start | bytes 294920 | tf_op jit(solution)/shard_map/ppermute | solution.py:437
  19.7 24.3 %copy-start.4 = (bf16[256,128]{1,0:T(8,128)(2,1)S(1)}, bf16[256,128]{1,0:T(8,128)(2,1)}, u32[]{:S(2)}) copy-start(bf16[256,128]{1,0:T(8,128)(2,1)} %w_out.1) | copy-start | bytes 196612
  19.7 24.3 %copy-start.6 = (bf16[64,256]{1,0:T(8,128)(2,1)S(1)}, bf16[64,256]{1,0:T(8,128)(2,1)}, u32[]{:S(2)}) copy-start(bf16[64,256]{1,0:T(8,128)(2,1)} %w_in.1) | copy-start | bytes 98308
